TPU v7x, 128 devices: a whole 4x4x4 slice. The times are simulated.
128 devices in a mesh: gx: 8 (over z, core), gy: 16 (over x, y).
Axes of the slice: x: 4, y: 4, z: 4, core: 2. Of those that a mesh axis runs over, the one named last changes fastest.
Arguments:
- features: bfloat16 [8, 16, 16, 8, 8, 8, 128], P('gx', 'gy'), may hold values from -6 to 6
- cotangent: bfloat16 [8, 16, 16, 8, 8, 8, 128], P('gx', 'gy'), may hold values from -6 to 6
- kernel_weight: bfloat16 [3, 3, 3, 128, 128], replicated, may hold values from -0.109375 to 0.109375
- conv_bias: float32 [128], replicated, may hold values from -3 to 3
- send_lists: int32 [8, 16, 8, 4], P('gx', 'gy'), may hold values from 0 to 16, as said below
- kernel_map: int32 [8, 16, 16, 27], P('gx', 'gy'), may hold values from 0 to 48, as said below
Outputs:
- activated: bfloat16 [8, 16, 16, 8, 8, 8, 128], P('gx', 'gy')
- input_grad: bfloat16 [8, 16, 16, 8, 8, 8, 128], P('gx', 'gy')
- weight_grad: float32 [3, 3, 3, 128, 128], replicated
- bias_grad: float32 [128], replicated
Inputs may be any that keep to these rules, and one draw needn't show every extreme that they name: send_lists[i, j, k] names distinct own bricks (0 to 15) in its first 1 to 4 slots and 16 in the rest; it is all 16 where region (i+dx, j+dy) of direction k lies outside the grid. In every draw some interior region receives 4 named bricks in all 8 lists that reach it. kernel_map[i, j, b, 13] = b. Other entries name an own brick (below 16), a received slot 16 + 4 k + r whose brick is named (r below the count named in the list k of region (i-dx, j-dy)), or 48, an absent brick. Every named received slot appears somewhere in the region's map.
All inputs are finite; a program needn't handle non-finite values.
Results may differ from a plain program's by a relative error of at most 0.008.
Values may be sent and summed in bfloat16 or wider, within the bound.
A program may use at most 128 MiB of HBM per device.

v0:
```python
import math

import jax
import jax.numpy as jnp
import numpy as np
from jax import lax
from jax.sharding import PartitionSpec as P

DIRECTIONS = ((-1, -1), (-1, 0), (-1, 1), (0, -1), (0, 1), (1, -1), (1, 0), (1, 1))


def passed_along(block, axis, distance):
    devices = range(lax.axis_size(axis))
    route = [(i - distance, i) for i in devices if i - distance in devices]
    return lax.ppermute(block, axis, route)


def brick_faces(bricks):
    last_idx = bricks.shape[1] - 1
    return jnp.stack(
        [
            bricks[:, 0],
            bricks[:, last_idx],
            bricks[:, :, 0],
            bricks[:, :, last_idx],
            bricks[:, :, :, 0],
            bricks[:, :, :, last_idx],
        ],
        axis=1,
    )


def sign_of(coord, edge_len):
    if coord == 0:
        return -1
    if coord == edge_len + 1:
        return 1
    return 0


def face_index(sign_val, coord, edge_len):
    if sign_val < 0:
        return edge_len - 1
    if sign_val > 0:
        return 0
    return coord - 1


def rim_tables(edge_len):
    side = edge_len + 2
    cells = side * side * side
    centre_mask = np.zeros((cells,), np.bool_)
    offset_col = np.zeros((cells,), np.int32)
    inner_pos = np.zeros((cells,), np.int32)
    face_pos = np.zeros((cells,), np.int32)
    square = edge_len * edge_len
    for cell in range(cells):
        p, q, r = (cell // (side * side), cell // side % side, cell % side)
        a, b, c = (sign_of(p, edge_len), sign_of(q, edge_len), sign_of(r, edge_len))
        offset_col[cell] = 9 * (a + 1) + 3 * (b + 1) + (c + 1)
        if a == 0 and b == 0 and (c == 0):
            centre_mask[cell] = True
            inner_pos[cell] = ((p - 1) * edge_len + (q - 1)) * edge_len + (r - 1)
            continue
        if a != 0:
            face_id = 1 if a < 0 else 0
            first, second = (face_index(b, q, edge_len), face_index(c, r, edge_len))
        elif b != 0:
            face_id = 3 if b < 0 else 2
            first, second = (p - 1, face_index(c, r, edge_len))
        else:
            face_id = 5 if c < 0 else 4
            first, second = (p - 1, q - 1)
        face_pos[cell] = face_id * square + first * edge_len + second
    return (centre_mask, offset_col, inner_pos, face_pos)


def assemble(volume, face_table, brick_map):
    brick_count = volume.shape[0]
    edge_len = volume.shape[1]
    channels = volume.shape[4]
    side = edge_len + 2
    cube = edge_len * edge_len * edge_len
    square = edge_len * edge_len
    centre_mask, offset_col, inner_pos, face_pos = rim_tables(edge_len)
    entries = jnp.take(brick_map, jnp.asarray(offset_col), axis=1).astype(jnp.int32)
    brick_ids = jnp.arange(brick_count, dtype=jnp.int32)[:, None]
    own_rows = brick_ids * cube + jnp.asarray(inner_pos)[None, :]
    rim_rows = brick_count * cube + entries * (6 * square) + jnp.asarray(face_pos)[None, :]
    row_ids = jnp.where(jnp.asarray(centre_mask)[None, :], own_rows, rim_rows).astype(jnp.int32)
    pool = jnp.concatenate([volume.reshape(-1, channels), face_table.reshape(-1, channels)], axis=0)
    gathered = jnp.take(pool, row_ids.reshape(-1), axis=0)
    return gathered.reshape(brick_count, side, side, side, channels)


def conv_valid(padded, kernel):
    return lax.conv_general_dilated(
        padded,
        kernel,
        (1, 1, 1),
        "VALID",
        dimension_numbers=("NDHWC", "DHWIO", "NDHWC"),
        preferred_element_type=jnp.float32,
    )


def weight_terms(padded, slope_grad):
    edge_len = slope_grad.shape[1]
    channels = slope_grad.shape[4]
    flat_slope = slope_grad.reshape(-1, channels)
    partials = []
    for o in range(27):
        a, b, c = (o // 9, o // 3 % 3, o % 3)
        window = padded[:, a : a + edge_len, b : b + edge_len, c : c + edge_len].reshape(
            -1, channels
        )
        partials.append(
            lax.dot_general(
                window, flat_slope, (((0,), (0,)), ((), ())), preferred_element_type=jnp.float32
            )
        )
    return jnp.stack(partials).reshape(3, 3, 3, channels, channels)


def deliver(outgoing):
    columns_count = lax.axis_size("gy")
    arrived = []
    for k in range(8):
        shift_by = DIRECTIONS[k][0] * columns_count + DIRECTIONS[k][1]
        arrived.append(passed_along(outgoing[k], ("gx", "gy"), shift_by))
    return jnp.stack(arrived)


def neighbour_table(volume, send_list):
    own_faces = brick_faces(volume)
    face_shape = own_faces.shape[1:]
    source = jnp.concatenate([volume, jnp.zeros((1,) + volume.shape[1:], volume.dtype)], axis=0)
    arrived = deliver(source[send_list])
    incoming = brick_faces(arrived.reshape((-1,) + volume.shape[1:]))
    return jnp.concatenate(
        [own_faces, incoming, jnp.zeros((1,) + face_shape, own_faces.dtype)], axis=0
    )


def shards(features, cotangent, kernel_weight, conv_bias, send_lists, kernel_map):
    volume = features[0, 0]
    send_list = send_lists[0, 0]
    brick_map = kernel_map[0, 0]
    padded = assemble(volume, neighbour_table(volume, send_list), brick_map)
    linear = conv_valid(padded, kernel_weight) + conv_bias
    logistic = jax.nn.sigmoid(linear)
    activated = (linear * logistic).astype(jnp.bfloat16)
    slope_grad = (
        cotangent[0, 0].astype(jnp.float32) * logistic * (1.0 + linear * (1.0 - logistic))
    ).astype(jnp.bfloat16)
    grad_padded = assemble(slope_grad, neighbour_table(slope_grad, send_list), brick_map)
    flipped = jnp.transpose(kernel_weight[::-1, ::-1, ::-1], (0, 1, 2, 4, 3))
    input_grad = conv_valid(grad_padded, flipped).astype(jnp.bfloat16)
    weight_part = weight_terms(padded, slope_grad)
    bias_part = jnp.sum(slope_grad, axis=(0, 1, 2, 3), dtype=jnp.float32)
    weight_total, bias_total = lax.psum((weight_part, bias_part), ("gx", "gy"))
    edge_len = volume.shape[1]
    total_voxels = (
        lax.axis_size("gx") * lax.axis_size("gy") * volume.shape[0] * edge_len * edge_len * edge_len
    )
    factor = 1.0 / math.sqrt(total_voxels)
    return (
        activated[None, None],
        input_grad[None, None],
        weight_total * factor,
        bias_total * factor,
    )


def solution(mesh):
    return jax.shard_map(
        shards,
        mesh=mesh,
        in_specs=(
            P("gx", "gy", None, None, None, None, None),
            P("gx", "gy", None, None, None, None, None),
            P(),
            P(),
            P("gx", "gy", None, None),
            P("gx", "gy", None, None),
        ),
        out_specs=(
            P("gx", "gy", None, None, None, None, None),
            P("gx", "gy", None, None, None, None, None),
            P(),
            P(),
        ),
        check_vma=False,
    )
```

profile of v0, /device:TPU:1, one launch (start us, length us, event | category | flops | bytes accessed | tf_op | source)
XLA Modules:
  0.0 490.1 jit_solution(15078585050110940367)
XLA Ops:
  11.7 4.7 gather_fusion
  16.4 4.5 fusion.54
  28.3 5.6 %collective-permute-start.3 = (bf16[4,8,8,8,128]{4,2,1,3,0:T(8,128)(2,1)}, bf16[4,8,8,8,128]{4,2,1,3,0:T(8,128)(2,1)}, u32[]{:S(2)}, u32[]{:S(2)}) collective-permute-start(bf16[4,8,8,8,128]{4,2,1,3,0:T(8,128)(2,1)} %get-tuple-element.43), channel_id=1, source_target_pairs={{1,0},{2,1},{3,2},{4,3},{5,4},{6,5},{7,6},{8,7},{9,8},{10,9},{11,1... | collective-permute-start | bytes 1572872 | tf_op jit(solution)/shard_map/ppermute | solution.py:15
  38.6 4.0 gather_fusion.2
  54.5 9.5 %collective-permute-start.5 = (bf16[4,8,8,8,128]{4,2,1,3,0:T(8,128)(2,1)S(1)}, bf16[4,8,8,8,128]{4,2,1,3,0:T(8,128)(2,1)S(1)}, u32[]{:S(2)}, u32[]{:S(2)}) collective-permute-start(bf16[4,8,8,8,128]{4,2,1,3,0:T(8,128)(2,1)S(1)} %copy-done.10), channel_id=1, source_target_pairs={{0,15},{1,16},{2,17},{3,18},{4,19},{5,20},{6,21},{7,22},{8,23},{9,... | collective-permute-start | bytes 1572872 | tf_op jit(solution)/shard_map/ppermute | solution.py:15
  65.2 7.3 %collective-permute-start.6 = (bf16[4,8,8,8,128]{4,2,1,3,0:T(8,128)(2,1)S(1)}, bf16[4,8,8,8,128]{4,2,1,3,0:T(8,128)(2,1)S(1)}, u32[]{:S(2)}, u32[]{:S(2)}) collective-permute-start(bf16[4,8,8,8,128]{4,2,1,3,0:T(8,128)(2,1)S(1)} %copy-done.9), channel_id=1, source_target_pairs={{0,16},{1,17},{2,18},{3,19},{4,20},{5,21},{6,22},{7,23},{8,24},{9,... | collective-permute-start | bytes 1572872 | tf_op jit(solution)/shard_map/ppermute | solution.py:15
  78.7 5.6 %collective-permute-done.7 = bf16[4,8,8,8,128]{4,2,1,3,0:T(8,128)(2,1)S(1)} collective-permute-done((bf16[4,8,8,8,128]{4,2,1,3,0:T(8,128)(2,1)S(1)}, bf16[4,8,8,8,128]{4,2,1,3,0:T(8,128)(2,1)S(1)}, u32[]{:S(2)}, u32[]{:S(2)}) %collective-permute-start.7) | collective-permute-done | bytes 524320 | tf_op jit(solution)/shard_map/ppermute | solution.py:15
  90.1 25.3 %pad_maximum_fusion = bf16[27008,128]{1,0:T(8,128)(2,1)} fusion(bf16[18816,128]{1,0:T(8,128)(2,1)S(1)} %bitcast.412, bf16[8192,128]{1,0:T(8,128)(2,1)S(1)} %bitcast.420), kind=kLoop, calls=%fused_computation.5 | loop fusion | flops 13828096 | bytes 13828096 | tf_op jit(solution)/shard_map/concatenate | solution.py:91
  115.4 34.3 %gather_fusion.3 = bf16[16000,128]{1,0:T(8,128)(2,1)} fusion(bf16[27008,128]{1,0:T(8,128)(2,1)} %pad_maximum_fusion, s32[16384]{0:T(1024)S(1)} %pad_clamp_fusion), kind=kCustom, calls=%fused_computation.1.clone | custom fusion | bytes 8256000 | tf_op jit(solution)/shard_map/jit(_take)/gather | solution.py:92
  149.7 11.8 %broadcast_select_fusion.1 = bf16[16000,128]{1,0:T(8,128)(2,1)} fusion(bf16[16000,128]{1,0:T(8,128)(2,1)} %gather_fusion.3, pred[16000]{0:T(1024)(128)(4,1)S(1)} %compare_and_fusion), kind=kLoop, calls=%fused_computation.18 | loop fusion | flops 2048000 | bytes 8208000 | tf_op jit(solution)/shard_map/jit(_take)/select_n | solution.py:92
  161.6 8.7 %reshape.121 = bf16[16,10,10,10,128]{4,3,2,1,0:T(8,128)(2,1)} reshape(bf16[16000,128]{1,0:T(8,128)(2,1)} %broadcast_select_fusion.1) | data formatting | bytes 8192000 | tf_op jit(solution)/shard_map/reshape | solution.py:93
  170.2 7.7 %copy.173 = bf16[16,10,10,10,128]{4,0,3,2,1:T(8,128)(2,1)S(1)} copy(bf16[16,10,10,10,128]{4,3,2,1,0:T(8,128)(2,1)} %reshape.121) | data formatting | bytes 8192000 | tf_op jit(solution)/shard_map/reshape | solution.py:93
  178.0 18.6 %convert_reduce_fusion = (f32[128]{0:T(128)}, bf16[16,8,8,8,128]{4,0,3,2,1:T(8,128)(2,1)S(1)}, bf16[1,1,16,8,8,8,128]{6,2,5,4,3,1,0:T(8,128)(2,1)}) fusion(f32[128]{0:T(128)S(1)} %copy-done.28, bf16[1,1,16,8,8,8,128]{6,5,4,3,2,1,0:T(8,128)(2,1)S(1)} %copy-done.27, bf16[16,10,10,10,128]{4,0,3,2,1:T(8,128)(2,1)S(1)} %copy.173, ...), kind=kOutput, calls=%fused_computation.12 | convolution fusion | flops 7263485952 | bytes 11273216 | tf_op jit(solution)/shard_map/conv_general_dilated | solution.py:97
  229.2 4.8 gather_fusion.1
  234.0 4.4 fusion.51
  246.9 85.8 %psum.15 = f32[128]{0:T(128)S(1)} all-reduce(f32[128]{0:T(128)S(1)} %copy-done.29), channel_id=1, replica_groups=mesh['gx'=8,'gy'=16] {'gx','gy'}, use_global_device_ids=true, to_apply=%region_2.5 | all-reduce | flops 128 | bytes 1024 | tf_op jit(solution)/shard_map/psum | solution.py:161
  335.3 5.1 %collective-permute-start.11 = (bf16[4,8,8,8,128]{4,3,2,1,0:T(8,128)(2,1)S(1)}, bf16[4,8,8,8,128]{4,3,2,1,0:T(8,128)(2,1)S(1)}, u32[]{:S(2)}, u32[]{:S(2)}) collective-permute-start(bf16[4,8,8,8,128]{4,3,2,1,0:T(8,128)(2,1)S(1)} %copy-done.14), channel_id=1, source_target_pairs={{1,0},{2,1},{3,2},{4,3},{5,4},{6,5},{7,6},{8,7},{9,8},{10,9},{11,1... | collective-permute-start | bytes 1572872 | tf_op jit(solution)/shard_map/ppermute | solution.py:15
  344.4 7.3 %collective-permute-start.13 = (bf16[4,8,8,8,128]{4,3,2,1,0:T(8,128)(2,1)S(1)}, bf16[4,8,8,8,128]{4,3,2,1,0:T(8,128)(2,1)S(1)}, u32[]{:S(2)}, u32[]{:S(2)}) collective-permute-start(bf16[4,8,8,8,128]{4,3,2,1,0:T(8,128)(2,1)S(1)} %copy-done.12), channel_id=1, source_target_pairs={{0,15},{1,16},{2,17},{3,18},{4,19},{5,20},{6,21},{7,22},{8,23},{9,... | collective-permute-start | bytes 1572872 | tf_op jit(solution)/shard_map/ppermute | solution.py:15
  363.5 13.8 %collective-permute-done.14 = bf16[4,8,8,8,128]{4,3,2,1,0:T(8,128)(2,1)S(1)} collective-permute-done((bf16[4,8,8,8,128]{4,3,2,1,0:T(8,128)(2,1)S(1)}, bf16[4,8,8,8,128]{4,3,2,1,0:T(8,128)(2,1)S(1)}, u32[]{:S(2)}, u32[]{:S(2)}) %collective-permute-start.14) | collective-permute-done | bytes 524320 | tf_op jit(solution)/shard_map/ppermute | solution.py:15
  380.9 25.4 %pad_maximum_fusion.1 = bf16[27008,128]{1,0:T(8,128)(2,1)} fusion(bf16[18816,128]{1,0:T(8,128)(2,1)S(1)} %bitcast.411, bf16[8192,128]{1,0:T(8,128)(2,1)S(1)} %bitcast.418), kind=kLoop, calls=%fused_computation.6 | loop fusion | flops 13828096 | bytes 13828096 | tf_op jit(solution)/shard_map/concatenate | solution.py:91
  406.2 34.3 %gather_fusion.4 = bf16[16000,128]{1,0:T(8,128)(2,1)} fusion(bf16[27008,128]{1,0:T(8,128)(2,1)} %pad_maximum_fusion.1, s32[16384]{0:T(1024)S(1)} %copy-done.7), kind=kCustom, calls=%fused_computation.2.clone | custom fusion | bytes 8256000 | tf_op jit(solution)/shard_map/jit(_take)/gather | solution.py:92
  440.5 11.8 %broadcast_select_fusion = bf16[16000,128]{1,0:T(8,128)(2,1)} fusion(bf16[16000,128]{1,0:T(8,128)(2,1)} %gather_fusion.4, pred[16000]{0:T(1024)(128)(4,1)S(1)} %copy-done.16), kind=kLoop, calls=%fused_computation.17 | loop fusion | flops 2048000 | bytes 8208000 | tf_op jit(solution)/shard_map/jit(_take)/select_n | solution.py:92
  452.4 8.3 %reshape.126 = bf16[16,10,10,10,128]{4,3,2,1,0:T(8,128)(2,1)} reshape(bf16[16000,128]{1,0:T(8,128)(2,1)} %broadcast_select_fusion) | data formatting | bytes 8192000 | tf_op jit(solution)/shard_map/reshape | solution.py:93
  460.6 17.6 %convert_bitcast_fusion = bf16[1,1,16,8,8,8,128]{6,2,5,4,3,1,0:T(8,128)(2,1)S(1)} fusion(bf16[3,3,3,128,128]{4,3,2,1,0:T(8,128)(2,1)S(1)} %copy-done, bf16[16,10,10,10,128]{4,3,2,1,0:T(8,128)(2,1)} %reshape.126), kind=kOutput, calls=%fused_computation.20 | convolution fusion | flops 7248805888 | bytes 7077888 | tf_op jit(solution)/shard_map/conv_general_dilated | solution.py:97
  (184 shorter events, 108.8 us)
Async XLA Ops:
  7.2 170.8 %copy-start = (bf16[3,3,3,128,128]{4,3,2,1,0:T(8,128)(2,1)S(1)}, bf16[3,3,3,128,128]{4,3,2,1,0:T(8,128)(2,1)}, u32[]{:S(2)}) copy-start(bf16[3,3,3,128,128]{4,3,2,1,0:T(8,128)(2,1)} %param.20) | copy-start | bytes 2654212
  7.2 472.9 %all-reduce.4.cloned.1.call-start = ((), (), s32[]{:S(2)}) async-start(), calls=%async_computation | async-start | bytes 3538944 | tf_op jit(solution)/shard_map/psum | solution.py:161
  20.9 33.6 %collective-permute-start = (bf16[4,8,8,8,128]{4,2,1,3,0:T(8,128)(2,1)}, bf16[4,8,8,8,128]{4,2,1,3,0:T(8,128)(2,1)}, u32[]{:S(2)}, u32[]{:S(2)}) collective-permute-start(bf16[4,8,8,8,128]{4,2,1,3,0:T(8,128)(2,1)} %get-tuple-element.46), channel_id=1, source_target_pairs={{17,0},{18,1},{19,2},{20,3},{21,4},{22,5},{23,6},{24,7},{25,8},{26... | collective-permute-start | bytes 1572872 | tf_op jit(solution)/shard_map/ppermute | solution.py:15
  22.4 42.8 %collective-permute-start.1 = (bf16[4,8,8,8,128]{4,2,1,3,0:T(8,128)(2,1)}, bf16[4,8,8,8,128]{4,2,1,3,0:T(8,128)(2,1)}, u32[]{:S(2)}, u32[]{:S(2)}) collective-permute-start(bf16[4,8,8,8,128]{4,2,1,3,0:T(8,128)(2,1)} %get-tuple-element.45), channel_id=1, source_target_pairs={{16,0},{17,1},{18,2},{19,3},{20,4},{21,5},{22,6},{23,7},{24,8},{25... | collective-permute-start | bytes 1572872 | tf_op jit(solution)/shard_map/ppermute | solution.py:15
  25.7 47.9 %collective-permute-start.2 = (bf16[4,8,8,8,128]{4,2,1,3,0:T(8,128)(2,1)}, bf16[4,8,8,8,128]{4,2,1,3,0:T(8,128)(2,1)}, u32[]{:S(2)}, u32[]{:S(2)}) collective-permute-start(bf16[4,8,8,8,128]{4,2,1,3,0:T(8,128)(2,1)} %get-tuple-element.44), channel_id=1, source_target_pairs={{15,0},{16,1},{17,2},{18,3},{19,4},{20,5},{21,6},{22,7},{23,8},{24... | collective-permute-start | bytes 1572872 | tf_op jit(solution)/shard_map/ppermute | solution.py:15
  28.3 47.8 %collective-permute-start.3 = (bf16[4,8,8,8,128]{4,2,1,3,0:T(8,128)(2,1)}, bf16[4,8,8,8,128]{4,2,1,3,0:T(8,128)(2,1)}, u32[]{:S(2)}, u32[]{:S(2)}) collective-permute-start(bf16[4,8,8,8,128]{4,2,1,3,0:T(8,128)(2,1)} %get-tuple-element.43), channel_id=1, source_target_pairs={{1,0},{2,1},{3,2},{4,3},{5,4},{6,5},{7,6},{8,7},{9,8},{10,9},{11,1... | collective-permute-start | bytes 1572872 | tf_op jit(solution)/shard_map/ppermute | solution.py:15
  33.9 43.3 %collective-permute-start.4 = (bf16[4,8,8,8,128]{4,2,1,3,0:T(8,128)(2,1)}, bf16[4,8,8,8,128]{4,2,1,3,0:T(8,128)(2,1)}, u32[]{:S(2)}, u32[]{:S(2)}) collective-permute-start(bf16[4,8,8,8,128]{4,2,1,3,0:T(8,128)(2,1)} %get-tuple-element.42), channel_id=1, source_target_pairs={{0,1},{1,2},{2,3},{3,4},{4,5},{5,6},{6,7},{7,8},{8,9},{9,10},{10,1... | collective-permute-start | bytes 1572872 | tf_op jit(solution)/shard_map/ppermute | solution.py:15
  48.5 25.1 %copy-start.8 = (bf16[4,8,8,8,128]{4,2,1,3,0:T(8,128)(2,1)S(1)}, bf16[4,8,8,8,128]{4,2,1,3,0:T(8,128)(2,1)}, u32[]{:S(2)}) copy-start(bf16[4,8,8,8,128]{4,2,1,3,0:T(8,128)(2,1)} %get-tuple-element.39) | copy-start | bytes 1572868
  50.4 99.4 %copy-start.15 = (pred[16000]{0:T(1024)(128)(4,1)}, pred[16000]{0:T(1024)(128)(4,1)S(1)}, u32[]{:S(2)}) copy-start(pred[16000]{0:T(1024)(128)(4,1)S(1)} %compare_and_fusion) | copy-start | bytes 48004
  54.4 61.0 %copy-start.6 = (s32[16384]{0:T(1024)}, s32[16384]{0:T(1024)S(1)}, u32[]{:S(2)}) copy-start(s32[16384]{0:T(1024)S(1)} %pad_clamp_fusion) | copy-start | bytes 196612
  54.5 33.5 %copy-start.23 = (bf16[49]{0:T(256)(128)(2,1)}, bf16[49]{0:T(256)(128)(2,1)S(1)}, u32[]{:S(2)}) copy-start(bf16[49]{0:T(256)(128)(2,1)S(1)} %pad.11.clone) | copy-start | bytes 298
  54.5 23.8 %collective-permute-start.5 = (bf16[4,8,8,8,128]{4,2,1,3,0:T(8,128)(2,1)S(1)}, bf16[4,8,8,8,128]{4,2,1,3,0:T(8,128)(2,1)S(1)}, u32[]{:S(2)}, u32[]{:S(2)}) collective-permute-start(bf16[4,8,8,8,128]{4,2,1,3,0:T(8,128)(2,1)S(1)} %copy-done.10), channel_id=1, source_target_pairs={{0,15},{1,16},{2,17},{3,18},{4,19},{5,20},{6,21},{7,22},{8,23},{9,... | collective-permute-start | bytes 1572872 | tf_op jit(solution)/shard_map/ppermute | solution.py:15
  65.2 13.5 %collective-permute-start.6 = (bf16[4,8,8,8,128]{4,2,1,3,0:T(8,128)(2,1)S(1)}, bf16[4,8,8,8,128]{4,2,1,3,0:T(8,128)(2,1)S(1)}, u32[]{:S(2)}, u32[]{:S(2)}) collective-permute-start(bf16[4,8,8,8,128]{4,2,1,3,0:T(8,128)(2,1)S(1)} %copy-done.9), channel_id=1, source_target_pairs={{0,16},{1,17},{2,18},{3,19},{4,20},{5,21},{6,22},{7,23},{8,24},{9,... | collective-permute-start | bytes 1572872 | tf_op jit(solution)/shard_map/ppermute | solution.py:15
  73.7 10.6 %collective-permute-start.7 = (bf16[4,8,8,8,128]{4,2,1,3,0:T(8,128)(2,1)S(1)}, bf16[4,8,8,8,128]{4,2,1,3,0:T(8,128)(2,1)S(1)}, u32[]{:S(2)}, u32[]{:S(2)}) collective-permute-start(bf16[4,8,8,8,128]{4,2,1,3,0:T(8,128)(2,1)S(1)} %copy-done.8), channel_id=1, source_target_pairs={{0,17},{1,18},{2,19},{3,20},{4,21},{5,22},{6,23},{7,24},{8,25},{9,... | collective-permute-start | bytes 1572872 | tf_op jit(solution)/shard_map/ppermute | solution.py:15
  238.4 106.0 %collective-permute-start.8 = (bf16[4,8,8,8,128]{4,3,2,1,0:T(8,128)(2,1)}, bf16[4,8,8,8,128]{4,3,2,1,0:T(8,128)(2,1)}, u32[]{:S(2)}, u32[]{:S(2)}) collective-permute-start(bf16[4,8,8,8,128]{4,3,2,1,0:T(8,128)(2,1)} %get-tuple-element.34), channel_id=1, source_target_pairs={{17,0},{18,1},{19,2},{20,3},{21,4},{22,5},{23,6},{24,7},{25,8},{26... | collective-permute-start | bytes 1572872 | tf_op jit(solution)/shard_map/ppermute | solution.py:15
  241.4 111.4 %collective-permute-start.9 = (bf16[4,8,8,8,128]{4,3,2,1,0:T(8,128)(2,1)}, bf16[4,8,8,8,128]{4,3,2,1,0:T(8,128)(2,1)}, u32[]{:S(2)}, u32[]{:S(2)}) collective-permute-start(bf16[4,8,8,8,128]{4,3,2,1,0:T(8,128)(2,1)} %get-tuple-element.33), channel_id=1, source_target_pairs={{16,0},{17,1},{18,2},{19,3},{20,4},{21,5},{22,6},{23,7},{24,8},{25... | collective-permute-start | bytes 1572872 | tf_op jit(solution)/shard_map/ppermute | solution.py:15
  245.0 110.9 %collective-permute-start.10 = (bf16[4,8,8,8,128]{4,3,2,1,0:T(8,128)(2,1)}, bf16[4,8,8,8,128]{4,3,2,1,0:T(8,128)(2,1)}, u32[]{:S(2)}, u32[]{:S(2)}) collective-permute-start(bf16[4,8,8,8,128]{4,3,2,1,0:T(8,128)(2,1)} %get-tuple-element.32), channel_id=1, source_target_pairs={{15,0},{16,1},{17,2},{18,3},{19,4},{20,5},{21,6},{22,7},{23,8},{24... | collective-permute-start | bytes 1572872 | tf_op jit(solution)/shard_map/ppermute | solution.py:15
  335.3 23.0 %collective-permute-start.11 = (bf16[4,8,8,8,128]{4,3,2,1,0:T(8,128)(2,1)S(1)}, bf16[4,8,8,8,128]{4,3,2,1,0:T(8,128)(2,1)S(1)}, u32[]{:S(2)}, u32[]{:S(2)}) collective-permute-start(bf16[4,8,8,8,128]{4,3,2,1,0:T(8,128)(2,1)S(1)} %copy-done.14), channel_id=1, source_target_pairs={{1,0},{2,1},{3,2},{4,3},{5,4},{6,5},{7,6},{8,7},{9,8},{10,9},{11,1... | collective-permute-start | bytes 1572872 | tf_op jit(solution)/shard_map/ppermute | solution.py:15
  340.4 20.0 %collective-permute-start.12 = (bf16[4,8,8,8,128]{4,3,2,1,0:T(8,128)(2,1)S(1)}, bf16[4,8,8,8,128]{4,3,2,1,0:T(8,128)(2,1)S(1)}, u32[]{:S(2)}, u32[]{:S(2)}) collective-permute-start(bf16[4,8,8,8,128]{4,3,2,1,0:T(8,128)(2,1)S(1)} %copy-done.13), channel_id=1, source_target_pairs={{0,1},{1,2},{2,3},{3,4},{4,5},{5,6},{6,7},{7,8},{8,9},{9,10},{10,1... | collective-permute-start | bytes 1572872 | tf_op jit(solution)/shard_map/ppermute | solution.py:15
  344.4 19.0 %collective-permute-start.13 = (bf16[4,8,8,8,128]{4,3,2,1,0:T(8,128)(2,1)S(1)}, bf16[4,8,8,8,128]{4,3,2,1,0:T(8,128)(2,1)S(1)}, u32[]{:S(2)}, u32[]{:S(2)}) collective-permute-start(bf16[4,8,8,8,128]{4,3,2,1,0:T(8,128)(2,1)S(1)} %copy-done.12), channel_id=1, source_target_pairs={{0,15},{1,16},{2,17},{3,18},{4,19},{5,20},{6,21},{7,22},{8,23},{9,... | collective-permute-start | bytes 1572872 | tf_op jit(solution)/shard_map/ppermute | solution.py:15
  352.8 24.4 %collective-permute-start.14 = (bf16[4,8,8,8,128]{4,3,2,1,0:T(8,128)(2,1)S(1)}, bf16[4,8,8,8,128]{4,3,2,1,0:T(8,128)(2,1)S(1)}, u32[]{:S(2)}, u32[]{:S(2)}) collective-permute-start(bf16[4,8,8,8,128]{4,3,2,1,0:T(8,128)(2,1)S(1)} %copy-done.11), channel_id=1, source_target_pairs={{0,16},{1,17},{2,18},{3,19},{4,20},{5,21},{6,22},{7,23},{8,24},{9,... | collective-permute-start | bytes 1572872 | tf_op jit(solution)/shard_map/ppermute | solution.py:15
  355.9 21.4 %collective-permute-start.15 = (bf16[4,8,8,8,128]{4,3,2,1,0:T(8,128)(2,1)S(1)}, bf16[4,8,8,8,128]{4,3,2,1,0:T(8,128)(2,1)S(1)}, u32[]{:S(2)}, u32[]{:S(2)}) collective-permute-start(bf16[4,8,8,8,128]{4,3,2,1,0:T(8,128)(2,1)S(1)} %get-tuple-element.27), channel_id=1, source_target_pairs={{0,17},{1,18},{2,19},{3,20},{4,21},{5,22},{6,23},{7,24},{8,25},{9,... | collective-permute-start | bytes 1572872 | tf_op jit(solution)/shard_map/ppermute | solution.py:15
  380.9 25.4 %copy-start.7 = (s32[16384]{0:T(1024)S(1)}, s32[16384]{0:T(1024)}, u32[]{:S(2)}) copy-start(s32[16384]{0:T(1024)} %copy-done.6) | copy-start | bytes 196612
  406.2 34.3 %copy-start.16 = (pred[16000]{0:T(1024)(128)(4,1)S(1)}, pred[16000]{0:T(1024)(128)(4,1)}, u32[]{:S(2)}) copy-start(pred[16000]{0:T(1024)(128)(4,1)} %copy-done.15) | copy-start | bytes 48004
  (23 other events, 231.7 us)
Sparse Core Ops, SparseCore 0:
  222.1 181.5 all-reduce.3
where the time goes:
time: 498 us; the launch traced here: 490 us
  local copies, waits for them, and re-layouts  167 us (34%)
  blocking collectives  85.8 us (17%)
  other arithmetic  84.6 us (17%)
  matrix products  57.6 us (12%)
  starting transfers between devices  55.9 us (11%)
  waiting for transfers between devices  24.5 us (5%)
  between operations  15.1 us (3%)
    psum x1, blocking collectives, shards(): weight_total, bias_total = lax.psum((weight_part, bias_part), ('gx', 'gy'))  85.8 us
    gather x2, local copies, waits for them, and re-layouts, assemble(): gathered = jnp.take(pool, row_ids.reshape(-1), axis=0)  68.6 us
    ppermute x16, starting transfers between devices, passed_along(): return lax.ppermute(block, axis, route)  55.8 us
    concatenate x2, other arithmetic, assemble(): jnp.concatenate([volume.reshape(-1, channels), face_table.reshape(-1, cha...  50.6 us
    conv_general_dilated x2, matrix products, conv_valid(): lax.conv_general_dilated(padded, kernel, (1, 1, 1), 'VALID', dimension_nu...  36.2 us
    unnamed x98, local copies, waits for them, and re-layouts  29.6 us
    reshape x3, local copies, waits for them, and re-layouts, assemble(): return gathered.reshape(brick_count, side, side, side, channels)  24.7 us
    select_n x3, other arithmetic, assemble(): gathered = jnp.take(pool, row_ids.reshape(-1), axis=0)  24.6 us
  transfers between devices with their start and end apart: 17, of which 5 were waited for; matrix products, arithmetic and copies ran while one was open for 32% of the time, Pallas kernels for 0%

commit v1 on v0

v1 whole, which is shorter than its diff:
```python
import functools
import math

import jax
import jax.numpy as jnp
from jax import lax
from jax.experimental import pallas as pl
from jax.experimental.pallas import tpu as pltpu
from jax.sharding import PartitionSpec as P

MESH = pl.DeviceIdType.MESH
F32, BF16 = jnp.float32, jnp.bfloat16
DIRECTIONS = ((-1, -1), (-1, 0), (-1, 1), (0, -1), (0, 1), (1, -1), (1, 0), (1, 1))
CH = 128
ENTRY = 52
SENT = 320
A_LOW, A_HIGH, E_LOW, E_HIGH, C_LOW, C_HIGH, EDGES = 0, 8, 16, 24, 32, 40, 48
SP, SQ, SR = 1600, 160, 16


def rows16(start):
    return pl.multiple_of(start, 16)


def natural_to_bricks(nat_ref, v32, put):
    def stage(b, _):
        block = nat_ref[b].astype(F32)
        for ae in range(64):
            v32[ae // 8, pl.ds((ae % 8) * 128 + b * 8, 8)] = block[ae * 8 : ae * 8 + 8]
        return 0

    lax.fori_loop(0, 16, stage, 0)

    def turn(ae, _):
        a, e = ae // 8, ae % 8
        for c in range(8):
            put(a, e, c, v32[a, pl.ds(e * 128 + c, 16, stride=8)])
        return 0

    lax.fori_loop(0, 64, turn, 0)


def bricks_to_natural(v32, nat_ref):
    def unstage(b, _):
        for ae in range(0, 64, 2):
            pair = [
                v32[(ae + k) // 8, pl.ds(((ae + k) % 8) * 128 + b * 8, 8)] for k in range(2)
            ]
            nat_ref[b, ae * 8 : ae * 8 + 16] = jnp.concatenate(pair, axis=0).astype(BF16)
        return 0

    lax.fori_loop(0, 16, unstage, 0)


def own_table(x32, t32, faces):
    def one(b, _):
        base = b * ENTRY
        for low, p in ((A_LOW, 1), (A_HIGH, 8)):
            for e in range(8):
                t32[base + low + e] = x32[pl.ds(p * SP + (1 + e) * SQ + SR + b, 8, stride=SR)]
        for low, q in ((E_LOW, 1), (E_HIGH, 8)):
            for a in range(8):
                t32[base + low + a] = x32[pl.ds((1 + a) * SP + q * SQ + SR + b, 8, stride=SR)]
        for low, r in ((C_LOW, 1), (C_HIGH, 8)):
            for a in range(8):
                t32[base + low + a] = x32[pl.ds((1 + a) * SP + SQ + r * SR + b, 8, stride=SQ)]
        for n, (q, r) in enumerate(((1, 1), (1, 8), (8, 1), (8, 8))):
            t32[base + EDGES + n] = x32[pl.ds(SP + q * SQ + r * SR + b, 8, stride=SP)]
        faces[b, 0:128] = t32[pl.ds(base, 16)].reshape(128, CH).astype(BF16)
        for n, low in enumerate((E_LOW, E_HIGH, C_LOW, C_HIGH)):
            lines = t32[pl.ds(base + low + 1, 6)].reshape(48, CH)
            faces[b, 128 + 48 * n : 176 + 48 * n] = lines.astype(BF16)
        return 0

    lax.fori_loop(0, 16, one, 0)


def received_table(received, t32, wide):
    def one(n, _):
        base = (16 + n) * ENTRY
        k, r = n // 4, n % 4
        sides = received[k, r, 0:128].astype(F32)
        wide[0:128] = sides
        t32[pl.ds(base, 16)] = sides.reshape(16, 8, CH)
        for m, low in enumerate((E_LOW, E_HIGH, C_LOW, C_HIGH)):
            lines = received[k, r, 128 + 48 * m : 176 + 48 * m].astype(F32)
            t32[pl.ds(base + low + 1, 6)] = lines.reshape(6, 8, CH)
            if m < 2:
                wide[136 + 64 * m : 184 + 64 * m] = lines
        for a, side in ((0, 0), (7, 64)):
            low, high = wide[side : side + 8], wide[side + 56 : side + 64]
            t32[base + E_LOW + a] = low
            t32[base + E_HIGH + a] = high
            wide[128 + 8 * a : 136 + 8 * a] = low
            wide[192 + 8 * a : 200 + 8 * a] = high
            t32[base + C_LOW + a] = wide[pl.ds(side, 8, stride=8)]
            t32[base + C_HIGH + a] = wide[pl.ds(side + 7, 8, stride=8)]
        for m, start in enumerate((128, 135, 192, 199)):
            t32[base + EDGES + m] = wide[pl.ds(start, 8, stride=8)]
        return 0

    lax.fori_loop(0, 32, one, 0)
    t32[pl.ds(48 * ENTRY, ENTRY)] = jnp.zeros((ENTRY, 8, CH), F32)


def rim(kmap, t32, x32, x):
    def one(b, _):
        for o in range(27):
            a, e, c = o // 9 - 1, o // 3 % 3 - 1, o % 3 - 1
            if a == e == c == 0:
                continue
            base = kmap[b, o] * ENTRY
            p, q, r = [1 + 8 * (s > 0) - (s < 0) for s in (a, e, c)]
            dest = p * SP + q * SQ + r * SR + b
            fe, fc = 7 * (e < 0), 7 * (c < 0)
            if a != 0:
                side = base + (A_HIGH if a < 0 else A_LOW)
                if e == 0 and c == 0:
                    for n in range(8):
                        x32[pl.ds(dest + n * SQ, 8, stride=SR)] = t32[side + n]
                elif c == 0:
                    x32[pl.ds(dest, 8, stride=SR)] = t32[side + fe]
                elif e == 0:
                    line = base + (C_HIGH if c < 0 else C_LOW) + 7 * (a < 0)
                    x32[pl.ds(dest, 8, stride=SQ)] = t32[line]
                else:
                    x32[pl.ds(dest, 1)] = t32[side + fe][fc : fc + 1]
            elif e != 0:
                side = base + (E_HIGH if e < 0 else E_LOW)
                if c == 0:
                    for n in range(8):
                        x32[pl.ds(dest + n * SP, 8, stride=SR)] = t32[side + n]
                else:
                    x32[pl.ds(dest, 8, stride=SP)] = t32[base + EDGES + 2 * (e < 0) + (c < 0)]
            else:
                side = base + (C_HIGH if c < 0 else C_LOW)
                for n in range(8):
                    x32[pl.ds(dest + n * SP, 8, stride=SQ)] = t32[side + n]
        return 0

    lax.fori_loop(0, 16, one, 0)

    def pack(p, q, r):
        x[p, q, r] = x32[pl.ds(rows16(p * SP + q * SQ + r * SR), 16)].astype(BF16)

    def line(q, _):
        for p in (0, 9):
            for r in range(10):
                pack(p, q, r)
        return 0

    lax.fori_loop(0, 10, line, 0)

    def ring(p, _):
        for q in (0, 9):
            for r in range(10):
                pack(p, q, r)
        for q in range(1, 9):
            for r in (0, 9):
                pack(p, q, r)
        return 0

    lax.fori_loop(1, 9, ring, 0)


def wide_weights(w, w2, back):
    zero = jnp.zeros((CH, CH), BF16)
    for e in range(3):
        for c in range(3):
            for k, j in ((0, 1), (3, 0)):
                w2[e, (c * 4 + k) * CH : (c * 4 + k + 1) * CH, j * CH : (j + 1) * CH] = zero
            for a in range(3):
                if back:
                    tap = w[(2 - a) * 9 + (2 - e) * 3 + 2 - c].astype(F32).T.astype(BF16)
                else:
                    tap = w[a * 9 + e * 3 + c]
                for j in range(2):
                    k = a + j
                    w2[e, (c * 4 + k) * CH : (c * 4 + k + 1) * CH, j * CH : (j + 1) * CH] = tap


def conv_pair(x, w2, i):
    acc = None
    for e in range(3):
        parts = [
            x[2 * i + k, e : e + 8, c : c + 8].reshape(1024, CH)
            for c in range(3)
            for k in range(4)
        ]
        term = jnp.dot(jnp.concatenate(parts, axis=1), w2[e], preferred_element_type=F32)
        acc = term if acc is None else acc + term
    return acc


def inside(i, j):
    return (i >= 0) & (i < lax.axis_size("gx")) & (j >= 0) & (j < lax.axis_size("gy"))


def greet_neighbours(barrier):
    i, j = lax.axis_index("gx"), lax.axis_index("gy")
    count = jnp.int32(0)
    for dx, dy in DIRECTIONS:
        there = inside(i + dx, j + dy)
        count += there.astype(jnp.int32)

        @pl.when(there)
        def _():
            pl.semaphore_signal(
                barrier, inc=1, device_id=(i + dx, j + dy), device_id_type=MESH
            )

    return count


def pack_lists(lists, faces, sending):
    for k in range(8):
        for r in range(4):
            sending[k, r] = faces[jnp.minimum(lists[k, r], 15)]


def halo_copy(k, sending, received, send_sem, recv_sem):
    i, j = lax.axis_index("gx"), lax.axis_index("gy")
    dx, dy = DIRECTIONS[k]
    return pltpu.make_async_remote_copy(
        src_ref=sending.at[k],
        dst_ref=received.at[k],
        send_sem=send_sem.at[k],
        recv_sem=recv_sem.at[k],
        device_id=(i + dx, j + dy),
        device_id_type=MESH,
    )


ORDER = (0, 2, 5, 7, 3, 4, 1, 6)


def start_halo(*halo):
    i, j = lax.axis_index("gx"), lax.axis_index("gy")
    for k in ORDER:
        dx, dy = DIRECTIONS[k]

        @pl.when(inside(i + dx, j + dy))
        def _():
            halo_copy(k, *halo).start()


def wait_halo(*halo):
    i, j = lax.axis_index("gx"), lax.axis_index("gy")
    for k in ORDER:
        dx, dy = DIRECTIONS[k]

        @pl.when(inside(i - dx, j - dy))
        def _():
            halo_copy(k, *halo).wait_recv()


def wait_halo_sent(*halo):
    i, j = lax.axis_index("gx"), lax.axis_index("gy")
    for k in ORDER:
        dx, dy = DIRECTIONS[k]

        @pl.when(inside(i + dx, j + dy))
        def _():
            halo_copy(k, *halo).wait_send()


def forward_kernel(
    vol, cot, w, bias, lists, kmap, act, slopes, x,
    v32, x32, t32, wide, ct, faces, sending, received, w2, acc, send_sem, recv_sem,
):
    halo = (sending, received, send_sem, recv_sem)
    barrier = pltpu.get_barrier_semaphore()
    count = greet_neighbours(barrier)

    def put_x(a, e, c, v):
        x32[pl.ds(rows16((1 + a) * SP + (1 + e) * SQ + (1 + c) * SR), 16)] = v
        x[1 + a, 1 + e, 1 + c] = v.astype(BF16)

    natural_to_bricks(vol, v32, put_x)
    own_table(x32, t32, faces)
    pack_lists(lists, faces, sending)
    pl.semaphore_wait(barrier, count)
    start_halo(*halo)

    def put_cot(a, e, c, v):
        ct[pl.ds(rows16((a * 64 + e * 8 + c) * 16), 16)] = v

    natural_to_bricks(cot, v32, put_cot)
    wide_weights(w, w2, False)
    wait_halo(*halo)
    received_table(received, t32, wide)
    rim(kmap, t32, x32, x)

    def pair(i, _):
        acc[...] = conv_pair(x, w2, i)
        for j in range(2):

            def finish(e, _):
                a = 2 * i + j
                linear = acc[pl.ds(rows16(e * 128), 128), j * CH : (j + 1) * CH] + bias[...]
                s = 1.0 / (1.0 + jnp.exp(-linear))
                activated = linear * s
                for c in range(8):
                    v32[a, pl.ds(e * 128 + c, 16, stride=8)] = activated[c * 16 : c * 16 + 16]
                slope = (
                    ct[pl.ds(rows16(a * 1024 + e * 128), 128)]
                    * s
                    * (1.0 + linear * (1.0 - s))
                )
                slopes[pl.ds((a * 8 + e) * 8, 8)] = slope.astype(BF16).reshape(8, 16, CH)
                return 0

            lax.fori_loop(0, 8, finish, 0)
        return 0

    lax.fori_loop(0, 4, pair, 0)
    bricks_to_natural(v32, act)
    wait_halo_sent(*halo)


def forward(vol, cot, w, bias, lists, kmap):
    vm = pl.BlockSpec(memory_space=pltpu.VMEM)
    sm = pl.BlockSpec(memory_space=pltpu.SMEM)
    return pl.pallas_call(
        forward_kernel,
        out_shape=(
            jax.ShapeDtypeStruct((16, 512, CH), BF16),
            jax.ShapeDtypeStruct((512, 16, CH), BF16),
            jax.ShapeDtypeStruct((10, 10, 10, 16, CH), BF16),
        ),
        in_specs=[vm, vm, vm, vm, sm, sm],
        out_specs=(vm, vm, vm),
        scratch_shapes=[
            pltpu.VMEM((8, 1024, CH), F32),
            pltpu.VMEM((16000, CH), F32),
            pltpu.VMEM((49 * ENTRY, 8, CH), F32),
            pltpu.VMEM((256, CH), F32),
            pltpu.VMEM((8192, CH), F32),
            pltpu.VMEM((16, SENT, CH), BF16),
            pltpu.VMEM((8, 4, SENT, CH), BF16),
            pltpu.VMEM((8, 4, SENT, CH), BF16),
            pltpu.VMEM((3, 12 * CH, 2 * CH), BF16),
            pltpu.VMEM((1024, 2 * CH), F32),
            pltpu.SemaphoreType.DMA((8,)),
            pltpu.SemaphoreType.DMA((8,)),
        ],
        compiler_params=pltpu.CompilerParams(
            collective_id=0, has_side_effects=True, vmem_limit_bytes=62 * 2**20
        ),
        name="forward",
    )(vol, cot, w, bias, lists, kmap)


ROWS = 3584
HALF = ROWS // 2
SHARE = HALF // 16


def place():
    i = lax.axis_index("gx")
    return i // 2, i % 2, lax.axis_index("gy")


def sibling_copy(src, dst, sems, n):
    z, core, j = place()
    return pltpu.make_async_remote_copy(
        src_ref=src, dst_ref=dst, send_sem=sems.at[0, n], recv_sem=sems.at[1, n],
        device_id=(2 * z + 1 - core, j), device_id_type=MESH,
    )


def plane_copy(src, dst, sems, d):
    z, core, j = place()
    return pltpu.make_async_remote_copy(
        src_ref=src, dst_ref=dst, send_sem=sems.at[0, d], recv_sem=sems.at[1, d],
        device_id=(2 * z + core, (j + d) % 16), device_id_type=MESH,
    )


def column_copy(src, dst, sems, d):
    z, core, j = place()
    return pltpu.make_async_remote_copy(
        src_ref=src, dst_ref=dst, send_sem=sems.at[0, d], recv_sem=sems.at[1, d],
        device_id=(2 * ((z + d) % 4) + core, j), device_id_type=MESH,
    )


def greet_summers(barrier):
    z, core, j = place()

    def greet(i, j):
        pl.semaphore_signal(barrier, inc=1, device_id=(i, j), device_id_type=MESH)

    greet(2 * z + 1 - core, j)
    for d in range(1, 16):
        greet(2 * z + core, (j + d) % 16)
    for d in range(1, 4):
        greet(2 * ((z + d) % 4) + core, j)
    return 19


def backward_kernel(
    x, slopes, w, lists, kmap, grad, total,
    v32, g, x32, t32, wide, faces, sending, received, w2, acc, gt,
    d32, d16, from_sibling, h32, h16, from_plane, column, share, gathered, whole,
    send_sem, recv_sem, sib_sems, out_sems, col_sems, in_sems,
):
    halo = (sending, received, send_sem, recv_sem)
    z, core, j = place()
    barrier = pltpu.get_barrier_semaphore()
    count = greet_neighbours(barrier) + greet_summers(barrier)

    def spread(ae, total):
        block = slopes[pl.ds(ae * 8, 8)]
        a, e = ae // 8, ae % 8
        g[1 + a, 1 + e, 1:9] = block
        wide = block.astype(F32).reshape(128, CH)
        x32[pl.ds(rows16((1 + a) * SP + (1 + e) * SQ + SR), 128)] = wide
        return total + wide

    sums = lax.fori_loop(0, 64, spread, jnp.zeros((128, CH), F32))
    d32[27 * CH :] = jnp.concatenate(
        [jnp.sum(sums, axis=0, keepdims=True), jnp.zeros((127, CH), F32)], axis=0
    )
    own_table(x32, t32, faces)
    pack_lists(lists, faces, sending)
    pl.semaphore_wait(barrier, count)
    start_halo(*halo)

    def turn(n, _):
        for m in range(8):
            block = slopes[pl.ds(n * 64 + m * 8, 8)].astype(F32).reshape(128, CH)
            gt[n // 2, pl.ds(rows16((n % 2) * CH), CH), m * 128 : m * 128 + 128] = (
                block.T.astype(BF16)
            )
        return 0

    lax.fori_loop(0, 8, turn, 0)

    def tap(t, _):
        e, c = t // 3, t % 3
        parts = [
            jnp.concatenate(
                [x[2 * i + k, pl.ds(e, 8), pl.ds(c, 8)].reshape(1024, CH) for i in range(4)],
                axis=0,
            )
            for k in range(4)
        ]
        terms = jnp.dot(
            jnp.concatenate([gt[i] for i in range(4)], axis=1),
            jnp.concatenate(parts, axis=1),
            preferred_element_type=F32,
        )
        for a in range(3):
            term = (
                terms[:CH, a * CH : (a + 1) * CH] + terms[CH:, (a + 1) * CH : (a + 2) * CH]
            )
            d32[pl.ds(rows16((a * 9 + t) * CH), CH)] = term.T
        return 0

    lax.fori_loop(0, 9, tap, 0)
    mine = pl.ds(rows16(core * HALF), HALF)
    other = pl.ds(rows16((1 - core) * HALF), HALF)
    d16[...] = d32[other].astype(BF16)
    sibling_copy(d16, from_sibling, sib_sems, 0).start()
    wide_weights(w, w2, True)
    wait_halo(*halo)
    received_table(received, t32, wide)
    rim(kmap, t32, x32, g)

    sibling_copy(d16, from_sibling, sib_sems, 0).wait()
    h32[...] = d32[mine] + from_sibling[...].astype(F32)
    h16[...] = h32[...].astype(BF16).reshape(16, SHARE, CH)
    for d in range(1, 16):
        plane_copy(h16.at[(j + d) % 16], from_plane.at[d - 1], out_sems, d).start()

    def conv(lo, hi):
        def pair(i, _):
            acc[...] = conv_pair(g, w2, i)
            for n in range(2):

                def finish(e, _):
                    for c in range(8):
                        v32[2 * i + n, pl.ds(e * 128 + c, 16, stride=8)] = acc[
                            pl.ds(rows16(e * 128 + c * 16), 16), n * CH : (n + 1) * CH
                        ]
                    return 0

                lax.fori_loop(0, 8, finish, 0)
            return 0

        lax.fori_loop(lo, hi, pair, 0)

    conv(0, 2)
    for d in range(1, 16):
        plane_copy(h16.at[(j + d) % 16], from_plane.at[d - 1], out_sems, d).wait()
    part = h32[pl.ds(rows16(j * SHARE), SHARE)]
    for d in range(1, 16):
        part = part + from_plane[d - 1].astype(F32)
    column[z] = part.astype(BF16)
    for d in range(1, 4):
        column_copy(column.at[z], column.at[z], col_sems, d).start()
    conv(2, 3)
    for d in range(1, 4):
        column_copy(column.at[z], column.at[z], col_sems, d).wait()
    part = column[0].astype(F32)
    for n in range(1, 4):
        part = part + column[n].astype(F32)
    voxels = lax.axis_size("gx") * lax.axis_size("gy") * 8192
    share[...] = (part * (1.0 / math.sqrt(voxels))).astype(BF16)
    gathered[j] = share[...]
    for d in range(1, 16):
        plane_copy(share, gathered.at[j], in_sems, d).start()
    conv(3, 4)
    for d in range(1, 16):
        plane_copy(share, gathered.at[j], in_sems, d).wait()
    sibling_copy(gathered, whole.at[core], sib_sems, 1).start()
    bricks_to_natural(v32, grad)
    total[pl.ds(rows16(core * HALF), HALF)] = gathered[...].reshape(HALF, CH).astype(F32)
    sibling_copy(gathered, whole.at[core], sib_sems, 1).wait()
    total[pl.ds(rows16((1 - core) * HALF), HALF)] = (
        whole[1 - core].reshape(HALF, CH).astype(F32)
    )
    wait_halo_sent(*halo)


def backward(x, slopes, w, lists, kmap):
    vm = pl.BlockSpec(memory_space=pltpu.VMEM)
    sm = pl.BlockSpec(memory_space=pltpu.SMEM)
    return pl.pallas_call(
        backward_kernel,
        out_shape=(
            jax.ShapeDtypeStruct((16, 512, CH), BF16),
            jax.ShapeDtypeStruct((ROWS, CH), F32),
        ),
        in_specs=[vm, vm, vm, sm, sm],
        out_specs=(vm, vm),
        scratch_shapes=[
            pltpu.VMEM((8, 1024, CH), F32),
            pltpu.VMEM((10, 10, 10, 16, CH), BF16),
            pltpu.VMEM((16000, CH), F32),
            pltpu.VMEM((49 * ENTRY, 8, CH), F32),
            pltpu.VMEM((256, CH), F32),
            pltpu.VMEM((16, SENT, CH), BF16),
            pltpu.VMEM((8, 4, SENT, CH), BF16),
            pltpu.VMEM((8, 4, SENT, CH), BF16),
            pltpu.VMEM((3, 12 * CH, 2 * CH), BF16),
            pltpu.VMEM((1024, 2 * CH), F32),
            pltpu.VMEM((4, 2 * CH, 1024), BF16),
            pltpu.VMEM((ROWS, CH), F32),
            pltpu.VMEM((HALF, CH), BF16),
            pltpu.VMEM((HALF, CH), BF16),
            pltpu.VMEM((HALF, CH), F32),
            pltpu.VMEM((16, SHARE, CH), BF16),
            pltpu.VMEM((15, SHARE, CH), BF16),
            pltpu.VMEM((4, SHARE, CH), BF16),
            pltpu.VMEM((SHARE, CH), BF16),
            pltpu.VMEM((16, SHARE, CH), BF16),
            pltpu.VMEM((2, 16, SHARE, CH), BF16),
            pltpu.SemaphoreType.DMA((8,)),
            pltpu.SemaphoreType.DMA((8,)),
            pltpu.SemaphoreType.DMA((2, 2)),
            pltpu.SemaphoreType.DMA((2, 16)),
            pltpu.SemaphoreType.DMA((2, 4)),
            pltpu.SemaphoreType.DMA((2, 16)),
        ],
        compiler_params=pltpu.CompilerParams(
            collective_id=1, has_side_effects=True, vmem_limit_bytes=62 * 2**20
        ),
        name="backward",
    )(x, slopes, w, lists, kmap)


def shards(features, cotangent, kernel_weight, conv_bias, send_lists, kernel_map):
    w = kernel_weight.reshape(27, CH, CH)
    lists, kmap = send_lists[0, 0], kernel_map[0, 0]
    act, slopes, x = forward(
        features.reshape(16, 512, CH),
        cotangent.reshape(16, 512, CH),
        w,
        conv_bias.reshape(1, CH),
        lists,
        kmap,
    )
    grad, total = backward(x, slopes, w, lists, kmap)
    return (
        act.reshape(features.shape),
        grad.reshape(features.shape),
        total[: 27 * CH].reshape(3, 3, 3, CH, CH),
        total[27 * CH],
    )


def solution(mesh):
    block = P("gx", "gy", None, None, None, None, None)
    return jax.shard_map(
        shards,
        mesh=mesh,
        in_specs=(block, block, P(), P(), P("gx", "gy", None, None), P("gx", "gy", None, None)),
        out_specs=(block, block, P(), P()),
        check_vma=False,
    )
```

time: 498 us -> 124 us (0.25); the launches traced: 490 us -> 123 us
  local copies, waits for them, and re-layouts: 167 us -> 9.15 us
  Pallas kernels: 0 us -> 113 us
  blocking collectives: 85.8 us -> 0 us
  other arithmetic: 84.6 us -> 0 us
  matrix products: 57.6 us -> 0 us
  starting transfers between devices: 55.9 us -> 0 us
  waiting for transfers between devices: 24.5 us -> 0 us
  between operations: 15.1 us -> 0.66 us
    pallas_call x0 -> x2, Pallas kernels: none -> 113 us  [the longest x1 64.8 us: backward(): pl.pallas_call(backward_kernel, out_shape=(jax.ShapeDtypeStruct((16, 512,...]
    psum x1 -> x0, blocking collectives: 85.8 us -> none  [shards(): weight_total, bias_total = lax.psum((weight_part, bias_part), ('gx', 'gy'))]
    gather x5 -> x0, local copies, waits for them, and re-layouts: 82.1 us -> none  [the longest x2 68.6 us: assemble(): gathered = jnp.take(pool, row_ids.reshape(-1), axis=0)]
    ppermute x16 -> x0, starting transfers between devices: 55.8 us -> none  [passed_along(): return lax.ppermute(block, axis, route)]
    concatenate x4 -> x0, other arithmetic: 53.2 us -> none  [the longest x2 50.6 us: assemble(): jnp.concatenate([volume.reshape(-1, channels), face_table.reshape(-1, cha...]
    conv_general_dilated x2 -> x0, matrix products: 36.2 us -> none  [conv_valid(): lax.conv_general_dilated(padded, kernel, (1, 1, 1), 'VALID', dimension_nu...]
    select_n x5 -> x0, other arithmetic: 27.1 us -> none  [the longest x3 24.6 us: assemble(): gathered = jnp.take(pool, row_ids.reshape(-1), axis=0)]
    reshape x4 -> x0, local copies, waits for them, and re-layouts: 26.2 us -> none  [the longest x3 24.7 us: assemble(): return gathered.reshape(brick_count, side, side, side, channels)]
  transfers between devices with their start and end apart: 17 -> 0, of which waited for: 5 -> 0; matrix products, arithmetic and copies ran while one was open for 32% -> 0% of each run, Pallas kernels for 0% -> 0%
where the time goes in v1:
time: 124 us; the launch traced here: 123 us
  Pallas kernels  113 us (91%)
  local copies, waits for them, and re-layouts  9.15 us (7%)
    pallas_call x1, Pallas kernels, backward(): pl.pallas_call(backward_kernel, out_shape=(jax.ShapeDtypeStruct((16, 512,...  64.8 us
    pallas_call x1, Pallas kernels, forward(): pl.pallas_call(forward_kernel, out_shape=(jax.ShapeDtypeStruct((16, 512,...  48.7 us
    unnamed x6, local copies, waits for them, and re-layouts  3.67 us
    slice x1, local copies, waits for them, and re-layouts, shards(): total[:27 * CH].reshape(3, 3, 3, CH, CH)  2.8 us

profile of v1, /device:TPU:1, one launch (start us, length us, event | category | flops | bytes accessed | tf_op | source)
XLA Modules:
  0.0 123.3 jit_solution(13112546280549439502)
XLA Ops:
  0.6 1.3 %copy.10.lists = s32[8,4]{1,0:T(8,128)} copy(s32[8,4]{0,1:T(4,128)} %bitcast.20) | data formatting | bytes 256 | tf_op jit(solution)/shard_map/squeeze | solution.py:576
  2.0 48.7 %forward.1 = (bf16[16,512,128]{2,1,0:T(8,128)(2,1)}, bf16[512,16,128]{2,1,0:T(8,128)(2,1)}, bf16[10,10,10,16,128]{4,3,2,1,0:T(8,128)(2,1)}) custom-call(bf16[16,512,128]{2,1,0:T(8,128)(2,1)} %bitcast.13, bf16[16,512,128]{2,1,0:T(8,128)(2,1)} %bitcast.14, bf16[27,128,128]{2,1,0:T(8,128)(2,1)} %bitcast.11, f32[1,128]{1,0:T(1,128)} %bitcast.21, ...), custom_call_target="tpu_custom_call" | custom-call | tf_op jit(solution)/shard_map/forward/pallas_call | solution.py:324
  50.7 64.8 %backward.1 = (bf16[16,512,128]{2,1,0:T(8,128)(2,1)}, f32[3584,128]{1,0:T(8,128)}) custom-call(bf16[10,10,10,16,128]{4,3,2,1,0:T(8,128)(2,1)} %get-tuple-element.10.x, bf16[512,16,128]{2,1,0:T(8,128)(2,1)} %get-tuple-element.11.slopes, bf16[27,128,128]{2,1,0:T(8,128)(2,1)} %bitcast.12, s32[8,4]{1,0:T(8,128)} %copy.10.lists, s32[16,27]{1,0:T(8,128)} %bitcast.19), custom_call_target="tpu_custom_call" | custom-call | tf_op jit(solution)/shard_map/backward/pallas_call | solution.py:530
  115.5 0.0 copy-start
  115.5 1.3 %slice_bitcast_fusion = f32[128]{0:T(128)} fusion(f32[3584,128]{1,0:T(8,128)} %get-tuple-element.13), kind=kLoop, calls=%fused_computation | loop fusion | bytes 1024 | tf_op jit(solution)/shard_map/squeeze | solution.py:590
  116.8 2.8 %slice.6 = f32[3456,128]{1,0:T(8,128)} slice(f32[3584,128]{1,0:T(8,128)} %get-tuple-element.13), slice={[0:3456], [0:128]} | slice | bytes 3538944 | tf_op jit(solution)/shard_map/slice | solution.py:589
  119.6 0.0 copy-done
  119.6 0.0 copy-start.1
  119.6 1.3 %copy.14 = bf16[1,1,16,8,8,8,128]{6,5,4,3,2,1,0:T(8,128)(2,1)} copy(bf16[1,1,16,8,8,8,128]{6,5,4,3,2,1,0:T(8,128)(2,1)S(1)} %bitcast.15) | data formatting | bytes 4194304
  120.9 1.0 copy-done.1
  122.0 1.3 %copy.15 = bf16[1,1,16,8,8,8,128]{6,5,4,3,2,1,0:T(8,128)(2,1)} copy(bf16[1,1,16,8,8,8,128]{6,5,4,3,2,1,0:T(8,128)(2,1)S(1)} %bitcast.16) | data formatting | bytes 4194304
Async XLA Ops:
  115.5 4.1 %copy-start = (bf16[16,512,128]{2,1,0:T(8,128)(2,1)S(1)}, bf16[16,512,128]{2,1,0:T(8,128)(2,1)}, u32[]{:S(2)}) copy-start(bf16[16,512,128]{2,1,0:T(8,128)(2,1)} %get-tuple-element.9) | copy-start | bytes 6291460
  119.6 2.3 %copy-start.1 = (bf16[16,512,128]{2,1,0:T(8,128)(2,1)S(1)}, bf16[16,512,128]{2,1,0:T(8,128)(2,1)}, u32[]{:S(2)}) copy-start(bf16[16,512,128]{2,1,0:T(8,128)(2,1)} %get-tuple-element.12) | copy-start | bytes 6291460

commit v2 on v1

--- a/solution.py
+++ b/solution.py
@@ -22,29 +22,30 @@
     return pl.multiple_of(start, 16)
 
 
-def natural_to_bricks(nat_ref, v32, put):
+def natural_to_bricks(nat_ref, stage_ref, put):
     def stage(b, _):
         block = nat_ref[b].astype(F32)
         for ae in range(64):
-            v32[ae // 8, pl.ds((ae % 8) * 128 + b * 8, 8)] = block[ae * 8 : ae * 8 + 8]
+            stage_ref[pl.ds(ae * 128 + pl.multiple_of(b * 8, 8), 8)] = block[
+                ae * 8 : ae * 8 + 8
+            ]
         return 0
 
     lax.fori_loop(0, 16, stage, 0)
 
     def turn(ae, _):
-        a, e = ae // 8, ae % 8
         for c in range(8):
-            put(a, e, c, v32[a, pl.ds(e * 128 + c, 16, stride=8)])
+            put(ae // 8, ae % 8, c, stage_ref[pl.ds(ae * 128 + c, 16, stride=8)])
         return 0
 
     lax.fori_loop(0, 64, turn, 0)
 
 
-def bricks_to_natural(v32, nat_ref):
+def bricks_to_natural(stage_ref, nat_ref):
     def unstage(b, _):
         for ae in range(0, 64, 2):
             pair = [
-                v32[(ae + k) // 8, pl.ds(((ae + k) % 8) * 128 + b * 8, 8)] for k in range(2)
+                stage_ref[pl.ds((ae + k) * 128 + pl.multiple_of(b * 8, 8), 8)] for k in range(2)
             ]
             nat_ref[b, ae * 8 : ae * 8 + 16] = jnp.concatenate(pair, axis=0).astype(BF16)
         return 0
@@ -103,7 +104,9 @@
     t32[pl.ds(48 * ENTRY, ENTRY)] = jnp.zeros((ENTRY, 8, CH), F32)
 
 
-def rim(kmap, t32, x32, x):
+def rim(kmap, t32, x32, planes, x):
+    a_planes, e_planes, c_planes = planes
+
     def one(b, _):
         for o in range(27):
             a, e, c = o // 9 - 1, o // 3 % 3 - 1, o % 3 - 1
@@ -141,42 +144,75 @@
     lax.fori_loop(0, 16, one, 0)
 
     def pack(p, q, r):
-        x[p, q, r] = x32[pl.ds(rows16(p * SP + q * SQ + r * SR), 16)].astype(BF16)
+        cell = x32[pl.ds(rows16(p * SP + q * SQ + r * SR), 16)].astype(BF16)
+        if x is not None:
+            x[p, q, r] = cell
+        return cell
 
     def line(q, _):
+        for side in range(2):
+            for r in range(10):
+                a_planes[side, q // 2, q % 2, r] = pack(9 * side, q, r)
+        return 0
+
+    lax.fori_loop(0, 10, line, 0)
+
+    def ring(p, _):
+        for side in range(2):
+            for r in range(10):
+                e_planes[side, p // 2, p % 2, r] = pack(p, 9 * side, r)
+            for q in range(1, 9):
+                c_planes[side, p // 2, p % 2, q] = pack(p, q, 9 * side)
+        return 0
+
+    lax.fori_loop(1, 9, ring, 0)
+
+
+def clear_rims(planes, x, g):
+    _, e_planes, c_planes = planes
+    row = jnp.zeros((10, 16, CH), BF16)
+    for side in range(2):
         for p in (0, 9):
-            for r in range(10):
-                pack(p, q, r)
-        return 0
-
-    lax.fori_loop(0, 10, line, 0)
-
-    def ring(p, _):
-        for q in (0, 9):
-            for r in range(10):
-                pack(p, q, r)
-        for q in range(1, 9):
-            for r in (0, 9):
-                pack(p, q, r)
-        return 0
-
-    lax.fori_loop(1, 9, ring, 0)
-
-
-def wide_weights(w, w2, back):
+            e_planes[side, p // 2, p % 2] = row
+            c_planes[side, p // 2, p % 2] = row
+        for p in range(1, 9):
+            for q in (0, 9):
+                c_planes[side, p // 2, p % 2, q] = row[0]
+
+    def clear(n, _):
+        for f in (x, g):
+            for side in (0, 9):
+                f[side, n] = row
+                f[n, side] = row
+                f[n, :, side] = row
+        return 0
+
+    lax.fori_loop(0, 10, clear, 0)
+
+
+def wide_weights(w, w2, wa, back):
     zero = jnp.zeros((CH, CH), BF16)
-    for e in range(3):
-        for c in range(3):
-            for k, j in ((0, 1), (3, 0)):
-                w2[e, (c * 4 + k) * CH : (c * 4 + k + 1) * CH, j * CH : (j + 1) * CH] = zero
-            for a in range(3):
+
+    def put(ref, n, c, k, j, tap):
+        ref[n, (c * 4 + k) * CH : (c * 4 + k + 1) * CH, j * CH : (j + 1) * CH] = tap
+
+    for c in range(3):
+        for k, j in ((0, 1), (3, 0)):
+            for n in range(3):
+                put(w2, n, c, k, j, zero)
+            for n in range(2):
+                put(wa, n, c, k, j, zero)
+    for a in range(3):
+        for e in range(3):
+            for c in range(3):
                 if back:
                     tap = w[(2 - a) * 9 + (2 - e) * 3 + 2 - c].astype(F32).T.astype(BF16)
                 else:
                     tap = w[a * 9 + e * 3 + c]
                 for j in range(2):
-                    k = a + j
-                    w2[e, (c * 4 + k) * CH : (c * 4 + k + 1) * CH, j * CH : (j + 1) * CH] = tap
+                    put(w2, e, c, a + j, j, tap)
+                    if a != 1:
+                        put(wa, a // 2, c, e + j, j, tap)
 
 
 def conv_pair(x, w2, i):
@@ -192,6 +228,51 @@
     return acc
 
 
+def inner_conv(x, w2, lin, lo, hi):
+    def pair(i, _):
+        result = conv_pair(x, w2, i)
+        for j in range(2):
+            lin[pl.ds(rows16((2 * i + j) * 1024), 1024)] = result[:, j * CH : (j + 1) * CH]
+        return 0
+
+    lax.fori_loop(lo, hi, pair, 0)
+
+
+def rim_conv(planes, w2, wa, lin):
+    a_planes, e_planes, c_planes = planes
+
+    def windows(ref, side):
+        parts = [
+            ref[side, k // 2 : k // 2 + 4, k % 2, s : s + 8].reshape(512, CH)
+            for s in range(3)
+            for k in range(4)
+        ]
+        return jnp.concatenate(parts, axis=1)
+
+    for side in range(2):
+        near = 7 * side
+        result = jnp.dot(windows(a_planes, side), wa[side], preferred_element_type=F32)
+        for i in range(4):
+            for j in range(2):
+                at = near * 1024 + (2 * i + j) * 128
+                lin[at : at + 128] += result[i * 128 : i * 128 + 128, j * CH : (j + 1) * CH]
+        result = jnp.dot(windows(e_planes, side), w2[2 * side], preferred_element_type=F32)
+        for i in range(4):
+            for j in range(2):
+                at = (2 * i + j) * 1024 + near * 128
+                lin[at : at + 128] += result[i * 128 : i * 128 + 128, j * CH : (j + 1) * CH]
+        taps = jnp.concatenate(
+            [w2[e, 2 * side * 4 * CH : (2 * side + 1) * 4 * CH] for e in range(3)], axis=0
+        )
+        result = jnp.dot(windows(c_planes, side), taps, preferred_element_type=F32)
+        for i in range(4):
+            for j in range(2):
+                for e in range(8):
+                    at = (2 * i + j) * 1024 + e * 128 + near * 16
+                    row = (i * 8 + e) * 16
+                    lin[at : at + 16] += result[row : row + 16, j * CH : (j + 1) * CH]
+
+
 def inside(i, j):
     return (i >= 0) & (i < lax.axis_size("gx")) & (j >= 0) & (j < lax.axis_size("gy"))
 
@@ -264,93 +345,6 @@
             halo_copy(k, *halo).wait_send()
 
 
-def forward_kernel(
-    vol, cot, w, bias, lists, kmap, act, slopes, x,
-    v32, x32, t32, wide, ct, faces, sending, received, w2, acc, send_sem, recv_sem,
-):
-    halo = (sending, received, send_sem, recv_sem)
-    barrier = pltpu.get_barrier_semaphore()
-    count = greet_neighbours(barrier)
-
-    def put_x(a, e, c, v):
-        x32[pl.ds(rows16((1 + a) * SP + (1 + e) * SQ + (1 + c) * SR), 16)] = v
-        x[1 + a, 1 + e, 1 + c] = v.astype(BF16)
-
-    natural_to_bricks(vol, v32, put_x)
-    own_table(x32, t32, faces)
-    pack_lists(lists, faces, sending)
-    pl.semaphore_wait(barrier, count)
-    start_halo(*halo)
-
-    def put_cot(a, e, c, v):
-        ct[pl.ds(rows16((a * 64 + e * 8 + c) * 16), 16)] = v
-
-    natural_to_bricks(cot, v32, put_cot)
-    wide_weights(w, w2, False)
-    wait_halo(*halo)
-    received_table(received, t32, wide)
-    rim(kmap, t32, x32, x)
-
-    def pair(i, _):
-        acc[...] = conv_pair(x, w2, i)
-        for j in range(2):
-
-            def finish(e, _):
-                a = 2 * i + j
-                linear = acc[pl.ds(rows16(e * 128), 128), j * CH : (j + 1) * CH] + bias[...]
-                s = 1.0 / (1.0 + jnp.exp(-linear))
-                activated = linear * s
-                for c in range(8):
-                    v32[a, pl.ds(e * 128 + c, 16, stride=8)] = activated[c * 16 : c * 16 + 16]
-                slope = (
-                    ct[pl.ds(rows16(a * 1024 + e * 128), 128)]
-                    * s
-                    * (1.0 + linear * (1.0 - s))
-                )
-                slopes[pl.ds((a * 8 + e) * 8, 8)] = slope.astype(BF16).reshape(8, 16, CH)
-                return 0
-
-            lax.fori_loop(0, 8, finish, 0)
-        return 0
-
-    lax.fori_loop(0, 4, pair, 0)
-    bricks_to_natural(v32, act)
-    wait_halo_sent(*halo)
-
-
-def forward(vol, cot, w, bias, lists, kmap):
-    vm = pl.BlockSpec(memory_space=pltpu.VMEM)
-    sm = pl.BlockSpec(memory_space=pltpu.SMEM)
-    return pl.pallas_call(
-        forward_kernel,
-        out_shape=(
-            jax.ShapeDtypeStruct((16, 512, CH), BF16),
-            jax.ShapeDtypeStruct((512, 16, CH), BF16),
-            jax.ShapeDtypeStruct((10, 10, 10, 16, CH), BF16),
-        ),
-        in_specs=[vm, vm, vm, vm, sm, sm],
-        out_specs=(vm, vm, vm),
-        scratch_shapes=[
-            pltpu.VMEM((8, 1024, CH), F32),
-            pltpu.VMEM((16000, CH), F32),
-            pltpu.VMEM((49 * ENTRY, 8, CH), F32),
-            pltpu.VMEM((256, CH), F32),
-            pltpu.VMEM((8192, CH), F32),
-            pltpu.VMEM((16, SENT, CH), BF16),
-            pltpu.VMEM((8, 4, SENT, CH), BF16),
-            pltpu.VMEM((8, 4, SENT, CH), BF16),
-            pltpu.VMEM((3, 12 * CH, 2 * CH), BF16),
-            pltpu.VMEM((1024, 2 * CH), F32),
-            pltpu.SemaphoreType.DMA((8,)),
-            pltpu.SemaphoreType.DMA((8,)),
-        ],
-        compiler_params=pltpu.CompilerParams(
-            collective_id=0, has_side_effects=True, vmem_limit_bytes=62 * 2**20
-        ),
-        name="forward",
-    )(vol, cot, w, bias, lists, kmap)
-
-
 ROWS = 3584
 HALF = ROWS // 2
 SHARE = HALF // 16
@@ -399,43 +393,98 @@
     return 19
 
 
-def backward_kernel(
-    x, slopes, w, lists, kmap, grad, total,
-    v32, g, x32, t32, wide, faces, sending, received, w2, acc, gt,
+def credit_neighbours(credit):
+    i, j = lax.axis_index("gx"), lax.axis_index("gy")
+    for dx, dy in DIRECTIONS:
+
+        @pl.when(inside(i - dx, j - dy))
+        def _():
+            pl.semaphore_signal(
+                credit, inc=1, device_id=(i - dx, j - dy), device_id_type=MESH
+            )
+
+
+def kernel(
+    vol, cot, w, bias, lists, kmap, act, grad, weight_total, bias_total,
+    nat, lin, x32, t32, wide, ct, faces, sending, received, x, g,
+    a_planes, e_planes, c_planes, w2, wa, gt,
     d32, d16, from_sibling, h32, h16, from_plane, column, share, gathered, whole,
-    send_sem, recv_sem, sib_sems, out_sems, col_sems, in_sems,
+    send_sem, recv_sem, sib_sems, out_sems, col_sems, in_sems, own_sems, credit,
 ):
     halo = (sending, received, send_sem, recv_sem)
+    planes = (a_planes, e_planes, c_planes)
     z, core, j = place()
+    take_vol = pltpu.make_async_copy(vol, nat, own_sems.at[0])
+    take_cot = pltpu.make_async_copy(cot, nat, own_sems.at[1])
+    give_act = pltpu.make_async_copy(nat, act, own_sems.at[2])
+    give_grad = pltpu.make_async_copy(nat, grad, own_sems.at[3])
+    take_vol.start()
     barrier = pltpu.get_barrier_semaphore()
-    count = greet_neighbours(barrier) + greet_summers(barrier)
-
-    def spread(ae, total):
-        block = slopes[pl.ds(ae * 8, 8)]
-        a, e = ae // 8, ae % 8
-        g[1 + a, 1 + e, 1:9] = block
-        wide = block.astype(F32).reshape(128, CH)
-        x32[pl.ds(rows16((1 + a) * SP + (1 + e) * SQ + SR), 128)] = wide
-        return total + wide
-
-    sums = lax.fori_loop(0, 64, spread, jnp.zeros((128, CH), F32))
-    d32[27 * CH :] = jnp.concatenate(
-        [jnp.sum(sums, axis=0, keepdims=True), jnp.zeros((127, CH), F32)], axis=0
-    )
+    neighbours = greet_neighbours(barrier)
+    summers = greet_summers(barrier)
+
+    def put_x(a, e, c, v):
+        x32[pl.ds(rows16((1 + a) * SP + (1 + e) * SQ + (1 + c) * SR), 16)] = v
+        x[1 + a, 1 + e, 1 + c] = v.astype(BF16)
+
+    take_vol.wait()
+    natural_to_bricks(nat, lin, put_x)
+    take_cot.start()
     own_table(x32, t32, faces)
     pack_lists(lists, faces, sending)
-    pl.semaphore_wait(barrier, count)
+    pl.semaphore_wait(barrier, neighbours + summers)
     start_halo(*halo)
 
-    def turn(n, _):
+    def put_cot(a, e, c, v):
+        ct[pl.ds(rows16((a * 64 + e * 8 + c) * 16), 16)] = v.astype(BF16)
+
+    take_cot.wait()
+    natural_to_bricks(nat, lin, put_cot)
+    wide_weights(w, w2, wa, False)
+    clear_rims(planes, x, g)
+    inner_conv(x, w2, lin, 0, 4)
+    wait_halo(*halo)
+    received_table(received, t32, wide)
+    credit_neighbours(credit)
+    rim(kmap, t32, x32, planes, x)
+    rim_conv(planes, w2, wa, lin)
+
+    def finish(ae, _):
+        a, e = ae // 8, ae % 8
+        rows = pl.ds(rows16(ae * 128), 128)
+        linear = lin[rows] + bias[...]
+        s = 1.0 / (1.0 + jnp.exp(-linear))
+        activated = linear * s
+        slope = ct[rows].astype(F32) * s * (1.0 + linear * (1.0 - s))
+        for c in range(8):
+            lin[pl.ds(ae * 128 + c, 16, stride=8)] = activated[c * 16 : c * 16 + 16]
+        x32[pl.ds(rows16((1 + a) * SP + (1 + e) * SQ + SR), 128)] = slope
+        g[1 + a, 1 + e, 1:9] = slope.astype(BF16).reshape(8, 16, CH)
+        return 0
+
+    lax.fori_loop(0, 64, finish, 0)
+    wait_halo_sent(*halo)
+    own_table(x32, t32, faces)
+    pack_lists(lists, faces, sending)
+    pl.semaphore_wait(credit, neighbours)
+    start_halo(*halo)
+
+    bricks_to_natural(lin, nat)
+    give_act.start()
+
+    def turn(n, sums):
         for m in range(8):
-            block = slopes[pl.ds(n * 64 + m * 8, 8)].astype(F32).reshape(128, CH)
+            block = g[1 + n, 1 + m, 1:9].astype(F32).reshape(128, CH)
             gt[n // 2, pl.ds(rows16((n % 2) * CH), CH), m * 128 : m * 128 + 128] = (
                 block.T.astype(BF16)
             )
-        return 0
-
-    lax.fori_loop(0, 8, turn, 0)
+            sums = sums + block
+        return sums
+
+    sums = lax.fori_loop(0, 8, turn, jnp.zeros((128, CH), F32))
+    d32[27 * CH :] = jnp.concatenate(
+        [jnp.sum(sums, axis=0, keepdims=True), jnp.zeros((127, CH), F32)], axis=0
+    )
 
     def tap(t, _):
         e, c = t // 3, t % 3
@@ -463,35 +512,15 @@
     other = pl.ds(rows16((1 - core) * HALF), HALF)
     d16[...] = d32[other].astype(BF16)
     sibling_copy(d16, from_sibling, sib_sems, 0).start()
-    wide_weights(w, w2, True)
-    wait_halo(*halo)
-    received_table(received, t32, wide)
-    rim(kmap, t32, x32, g)
+    wide_weights(w, w2, wa, True)
+    inner_conv(g, w2, lin, 0, 1)
 
     sibling_copy(d16, from_sibling, sib_sems, 0).wait()
     h32[...] = d32[mine] + from_sibling[...].astype(F32)
     h16[...] = h32[...].astype(BF16).reshape(16, SHARE, CH)
     for d in range(1, 16):
         plane_copy(h16.at[(j + d) % 16], from_plane.at[d - 1], out_sems, d).start()
-
-    def conv(lo, hi):
-        def pair(i, _):
-            acc[...] = conv_pair(g, w2, i)
-            for n in range(2):
-
-                def finish(e, _):
-                    for c in range(8):
-                        v32[2 * i + n, pl.ds(e * 128 + c, 16, stride=8)] = acc[
-                            pl.ds(rows16(e * 128 + c * 16), 16), n * CH : (n + 1) * CH
-                        ]
-                    return 0
-
-                lax.fori_loop(0, 8, finish, 0)
-            return 0
-
-        lax.fori_loop(lo, hi, pair, 0)
-
-    conv(0, 2)
+    inner_conv(g, w2, lin, 1, 4)
     for d in range(1, 16):
         plane_copy(h16.at[(j + d) % 16], from_plane.at[d - 1], out_sems, d).wait()
     part = h32[pl.ds(rows16(j * SHARE), SHARE)]
@@ -500,7 +529,8 @@
     column[z] = part.astype(BF16)
     for d in range(1, 4):
         column_copy(column.at[z], column.at[z], col_sems, d).start()
-    conv(2, 3)
+    wait_halo(*halo)
+    received_table(received, t32, wide)
     for d in range(1, 4):
         column_copy(column.at[z], column.at[z], col_sems, d).wait()
     part = column[0].astype(F32)
@@ -511,41 +541,65 @@
     gathered[j] = share[...]
     for d in range(1, 16):
         plane_copy(share, gathered.at[j], in_sems, d).start()
-    conv(3, 4)
+    rim(kmap, t32, x32, planes, None)
     for d in range(1, 16):
         plane_copy(share, gathered.at[j], in_sems, d).wait()
     sibling_copy(gathered, whole.at[core], sib_sems, 1).start()
-    bricks_to_natural(v32, grad)
-    total[pl.ds(rows16(core * HALF), HALF)] = gathered[...].reshape(HALF, CH).astype(F32)
+    whole[core] = gathered[...]
+    rim_conv(planes, w2, wa, lin)
+
+    def settle(ae, _):
+        block = lin[pl.ds(rows16(ae * 128), 128)]
+        for c in range(8):
+            lin[pl.ds(ae * 128 + c, 16, stride=8)] = block[c * 16 : c * 16 + 16]
+        return 0
+
+    lax.fori_loop(0, 64, settle, 0)
+    give_act.wait()
+    bricks_to_natural(lin, nat)
+    give_grad.start()
     sibling_copy(gathered, whole.at[core], sib_sems, 1).wait()
-    total[pl.ds(rows16((1 - core) * HALF), HALF)] = (
-        whole[1 - core].reshape(HALF, CH).astype(F32)
-    )
+    weight_total[0:HALF] = whole[0].reshape(HALF, CH).astype(F32)
+    last = whole[1].reshape(HALF, CH).astype(F32)
+    weight_total[HALF:] = last[: 27 * CH - HALF]
+    bias_total[...] = last[27 * CH - HALF : 27 * CH - HALF + 8]
     wait_halo_sent(*halo)
-
-
-def backward(x, slopes, w, lists, kmap):
+    give_grad.wait()
+
+
+def layer(vol, cot, w, bias, lists, kmap):
     vm = pl.BlockSpec(memory_space=pltpu.VMEM)
     sm = pl.BlockSpec(memory_space=pltpu.SMEM)
+    hbm = pl.BlockSpec(memory_space=pl.ANY)
+    field = pltpu.VMEM((10, 10, 10, 16, CH), BF16)
+    planes = pltpu.VMEM((2, 5, 2, 10, 16, CH), BF16)
     return pl.pallas_call(
-        backward_kernel,
+        kernel,
         out_shape=(
             jax.ShapeDtypeStruct((16, 512, CH), BF16),
-            jax.ShapeDtypeStruct((ROWS, CH), F32),
+            jax.ShapeDtypeStruct((16, 512, CH), BF16),
+            jax.ShapeDtypeStruct((27 * CH, CH), F32),
+            jax.ShapeDtypeStruct((8, CH), F32),
         ),
-        in_specs=[vm, vm, vm, sm, sm],
-        out_specs=(vm, vm),
+        in_specs=[hbm, hbm, vm, vm, sm, sm],
+        out_specs=(hbm, hbm, vm, vm),
         scratch_shapes=[
-            pltpu.VMEM((8, 1024, CH), F32),
-            pltpu.VMEM((10, 10, 10, 16, CH), BF16),
+            pltpu.VMEM((16, 512, CH), BF16),
+            pltpu.VMEM((8192, CH), F32),
             pltpu.VMEM((16000, CH), F32),
             pltpu.VMEM((49 * ENTRY, 8, CH), F32),
             pltpu.VMEM((256, CH), F32),
+            pltpu.VMEM((8192, CH), BF16),
             pltpu.VMEM((16, SENT, CH), BF16),
             pltpu.VMEM((8, 4, SENT, CH), BF16),
             pltpu.VMEM((8, 4, SENT, CH), BF16),
+            field,
+            field,
+            planes,
+            planes,
+            planes,
             pltpu.VMEM((3, 12 * CH, 2 * CH), BF16),
-            pltpu.VMEM((1024, 2 * CH), F32),
+            pltpu.VMEM((2, 12 * CH, 2 * CH), BF16),
             pltpu.VMEM((4, 2 * CH, 1024), BF16),
             pltpu.VMEM((ROWS, CH), F32),
             pltpu.VMEM((HALF, CH), BF16),
@@ -563,31 +617,30 @@
             pltpu.SemaphoreType.DMA((2, 16)),
             pltpu.SemaphoreType.DMA((2, 4)),
             pltpu.SemaphoreType.DMA((2, 16)),
+            pltpu.SemaphoreType.DMA((4,)),
+            pltpu.SemaphoreType.REGULAR,
         ],
         compiler_params=pltpu.CompilerParams(
-            collective_id=1, has_side_effects=True, vmem_limit_bytes=62 * 2**20
+            collective_id=0, has_side_effects=True, vmem_limit_bytes=63 * 2**20
         ),
-        name="backward",
-    )(x, slopes, w, lists, kmap)
+        name="layer",
+    )(vol, cot, w, bias, lists, kmap)
 
 
 def shards(features, cotangent, kernel_weight, conv_bias, send_lists, kernel_map):
-    w = kernel_weight.reshape(27, CH, CH)
-    lists, kmap = send_lists[0, 0], kernel_map[0, 0]
-    act, slopes, x = forward(
+    act, grad, weight_total, bias_total = layer(
         features.reshape(16, 512, CH),
         cotangent.reshape(16, 512, CH),
-        w,
+        kernel_weight.reshape(27, CH, CH),
         conv_bias.reshape(1, CH),
-        lists,
-        kmap,
-    )
-    grad, total = backward(x, slopes, w, lists, kmap)
+        send_lists[0, 0],
+        kernel_map[0, 0],
+    )
     return (
         act.reshape(features.shape),
         grad.reshape(features.shape),
-        total[: 27 * CH].reshape(3, 3, 3, CH, CH),
-        total[27 * CH],
+        weight_total.reshape(kernel_weight.shape),
+        bias_total[0],
     )
 
 

time: 124 us -> 106 us (0.85)
  the two profiles are of different devices: /device:TPU:1 before, /device:TPU:0 now
where the time goes in v2:
time: 106 us; the launch traced here: 105 us
  Pallas kernels  95.6 us (90%)
  local copies, waits for them, and re-layouts  9.27 us (9%)
    pallas_call x1, Pallas kernels, layer(): pl.pallas_call(kernel, out_shape=(jax.ShapeDtypeStruct((16, 512, CH), BF1...  95.6 us
    unnamed x7, local copies, waits for them, and re-layouts  6.73 us

profile of v2, /device:TPU:0, one launch (start us, length us, event | category | flops | bytes accessed | tf_op | source)
XLA Modules:
  0.0 105.5 jit_solution(2253575842529218427)
XLA Ops:
  0.6 1.3 %copy.10.lists = s32[8,4]{1,0:T(8,128)} copy(s32[8,4]{0,1:T(4,128)} %bitcast.18) | data formatting | bytes 256 | tf_op jit(solution)/shard_map/squeeze | solution.py:636
  2.0 95.6 %layer.1 = (bf16[16,512,128]{2,1,0:T(8,128)(2,1)}, bf16[16,512,128]{2,1,0:T(8,128)(2,1)}, f32[3456,128]{1,0:T(8,128)}, f32[8,128]{1,0:T(8,128)}) custom-call(bf16[16,512,128]{2,1,0:T(8,128)(2,1)} %bitcast.11, bf16[16,512,128]{2,1,0:T(8,128)(2,1)} %bitcast.12, bf16[27,128,128]{2,1,0:T(8,128)(2,1)} %bitcast.16, f32[1,128]{1,0:T(1,128)} %bitcast.19, ...), custom_call_target="tpu_custom_call" | custom-call | tf_op jit(solution)/shard_map/layer/pallas_call | solution.py:576
  97.5 1.2 %slice_bitcast_fusion = f32[128]{0:T(128)} fusion(f32[8,128]{1,0:T(8,128)} %get-tuple-element.11), kind=kLoop, calls=%fused_computation | loop fusion | bytes 1024 | tf_op jit(solution)/shard_map/squeeze | solution.py:643
  98.7 0.0 copy-start
  98.7 3.3 %copy.14 = bf16[1,1,16,8,8,8,128]{6,5,4,3,2,1,0:T(8,128)(2,1)} copy(bf16[1,1,16,8,8,8,128]{6,5,4,3,2,1,0:T(8,128)(2,1)} %bitcast.14) | data formatting | bytes 4194304
  102.0 0.0 copy-done
  102.0 0.0 copy-start.1
  102.0 1.3 %copy.15 = bf16[1,1,16,8,8,8,128]{6,5,4,3,2,1,0:T(8,128)(2,1)} copy(bf16[1,1,16,8,8,8,128]{6,5,4,3,2,1,0:T(8,128)(2,1)S(1)} %bitcast.13) | data formatting | bytes 4194304
  103.4 0.9 copy-done.1
  104.3 1.2 %copy.16 = f32[3,3,3,128,128]{4,3,2,1,0:T(8,128)} copy(f32[3,3,3,128,128]{4,3,2,1,0:T(8,128)S(1)} %bitcast.15) | data formatting | bytes 3538944
Async XLA Ops:
  98.7 3.3 %copy-start = (bf16[16,512,128]{2,1,0:T(8,128)(2,1)S(1)}, bf16[16,512,128]{2,1,0:T(8,128)(2,1)}, u32[]{:S(2)}) copy-start(bf16[16,512,128]{2,1,0:T(8,128)(2,1)} %get-tuple-element.9) | copy-start | bytes 6291460
  102.0 2.2 %copy-start.1 = (f32[3456,128]{1,0:T(8,128)S(1)}, f32[3456,128]{1,0:T(8,128)}, u32[]{:S(2)}) copy-start(f32[3456,128]{1,0:T(8,128)} %get-tuple-element.10) | copy-start | bytes 5308420

commit v3 on v2

--- a/solution.py
+++ b/solution.py
@@ -15,39 +15,41 @@
 ENTRY = 52
 SENT = 320
 A_LOW, A_HIGH, E_LOW, E_HIGH, C_LOW, C_HIGH, EDGES = 0, 8, 16, 24, 32, 40, 48
-SP, SQ, SR = 1600, 160, 16
+SP, SQ, SR = 1711, 171, 17
+LINE = 136
 
 
 def rows16(start):
     return pl.multiple_of(start, 16)
 
 
-def natural_to_bricks(nat_ref, stage_ref, put):
+def natural_to_bricks(nat, x32):
     def stage(b, _):
-        block = nat_ref[b].astype(F32)
+        block = nat[b].astype(F32)
         for ae in range(64):
-            stage_ref[pl.ds(ae * 128 + pl.multiple_of(b * 8, 8), 8)] = block[
-                ae * 8 : ae * 8 + 8
-            ]
+            at = (1 + ae // 8) * SP + (1 + ae % 8) * SQ + SR
+            x32[pl.ds(at + b, 8, stride=SR)] = block[ae * 8 : ae * 8 + 8]
         return 0
 
     lax.fori_loop(0, 16, stage, 0)
 
-    def turn(ae, _):
-        for c in range(8):
-            put(ae // 8, ae % 8, c, stage_ref[pl.ds(ae * 128 + c, 16, stride=8)])
-        return 0
-
-    lax.fori_loop(0, 64, turn, 0)
-
-
-def bricks_to_natural(stage_ref, nat_ref):
+
+def each_inner(x32, put):
+    def plane(a, _):
+        for e in range(8):
+            for c in range(8):
+                at = (1 + a) * SP + (1 + e) * SQ + (1 + c) * SR
+                put(a, e, c, x32[pl.ds(at, 16)].astype(BF16))
+        return 0
+
+    lax.fori_loop(0, 8, plane, 0)
+
+
+def bricks_to_natural(lin, nat):
     def unstage(b, _):
         for ae in range(0, 64, 2):
-            pair = [
-                stage_ref[pl.ds((ae + k) * 128 + pl.multiple_of(b * 8, 8), 8)] for k in range(2)
-            ]
-            nat_ref[b, ae * 8 : ae * 8 + 16] = jnp.concatenate(pair, axis=0).astype(BF16)
+            pair = [lin[pl.ds((ae + k) * LINE + b, 8, stride=17)] for k in range(2)]
+            nat[b, ae * 8 : ae * 8 + 16] = jnp.concatenate(pair, axis=0).astype(BF16)
         return 0
 
     lax.fori_loop(0, 16, unstage, 0)
@@ -144,7 +146,7 @@
     lax.fori_loop(0, 16, one, 0)
 
     def pack(p, q, r):
-        cell = x32[pl.ds(rows16(p * SP + q * SQ + r * SR), 16)].astype(BF16)
+        cell = x32[pl.ds(p * SP + q * SQ + r * SR, 16)].astype(BF16)
         if x is not None:
             x[p, q, r] = cell
         return cell
@@ -215,24 +217,34 @@
                         put(wa, a // 2, c, e + j, j, tap)
 
 
-def conv_pair(x, w2, i):
-    acc = None
-    for e in range(3):
-        parts = [
-            x[2 * i + k, e : e + 8, c : c + 8].reshape(1024, CH)
-            for c in range(3)
-            for k in range(4)
-        ]
-        term = jnp.dot(jnp.concatenate(parts, axis=1), w2[e], preferred_element_type=F32)
-        acc = term if acc is None else acc + term
-    return acc
-
-
-def inner_conv(x, w2, lin, lo, hi):
+def inner_conv(x, w2, wa, lin, lo, hi):
     def pair(i, _):
-        result = conv_pair(x, w2, i)
+        both = None
+        for e in range(3):
+            parts = [
+                x[2 * i + k, e : e + 8, c : c + 8].reshape(1024, CH)
+                for c in range(3)
+                for k in (1, 2)
+            ]
+            taps = jnp.concatenate(
+                [w2[e, (c * 4 + 1) * CH : (c * 4 + 3) * CH] for c in range(3)], axis=0
+            )
+            term = jnp.dot(jnp.concatenate(parts, axis=1), taps, preferred_element_type=F32)
+            both = term if both is None else both + term
         for j in range(2):
-            lin[pl.ds(rows16((2 * i + j) * 1024), 1024)] = result[:, j * CH : (j + 1) * CH]
+            plane = x[2 * i + 3 * j].reshape(5, 2, 10, 16, CH)
+            parts = [
+                plane[k // 2 : k // 2 + 4, k % 2, c : c + 8].reshape(512, CH)
+                for c in range(3)
+                for k in range(4)
+            ]
+            one = jnp.dot(jnp.concatenate(parts, axis=1), wa[j], preferred_element_type=F32)
+            for e in range(8):
+                at = pl.multiple_of(((2 * i + j) * 8 + e) * LINE, 8)
+                lin[pl.ds(at, 128)] = (
+                    both[e * 128 : e * 128 + 128, j * CH : (j + 1) * CH]
+                    + one[e // 2 * 128 : e // 2 * 128 + 128, e % 2 * CH : (e % 2 + 1) * CH]
+                )
         return 0
 
     lax.fori_loop(lo, hi, pair, 0)
@@ -254,12 +266,12 @@
         result = jnp.dot(windows(a_planes, side), wa[side], preferred_element_type=F32)
         for i in range(4):
             for j in range(2):
-                at = near * 1024 + (2 * i + j) * 128
+                at = (near * 8 + 2 * i + j) * LINE
                 lin[at : at + 128] += result[i * 128 : i * 128 + 128, j * CH : (j + 1) * CH]
         result = jnp.dot(windows(e_planes, side), w2[2 * side], preferred_element_type=F32)
         for i in range(4):
             for j in range(2):
-                at = (2 * i + j) * 1024 + near * 128
+                at = ((2 * i + j) * 8 + near) * LINE
                 lin[at : at + 128] += result[i * 128 : i * 128 + 128, j * CH : (j + 1) * CH]
         taps = jnp.concatenate(
             [w2[e, 2 * side * 4 * CH : (2 * side + 1) * 4 * CH] for e in range(3)], axis=0
@@ -268,7 +280,7 @@
         for i in range(4):
             for j in range(2):
                 for e in range(8):
-                    at = (2 * i + j) * 1024 + e * 128 + near * 16
+                    at = ((2 * i + j) * 8 + e) * LINE + near * 16
                     row = (i * 8 + e) * 16
                     lin[at : at + 16] += result[row : row + 16, j * CH : (j + 1) * CH]
 
@@ -296,7 +308,7 @@
 def pack_lists(lists, faces, sending):
     for k in range(8):
         for r in range(4):
-            sending[k, r] = faces[jnp.minimum(lists[k, r], 15)]
+            sending[k, r] = faces[jnp.minimum(lists[r, k], 15)]
 
 
 def halo_copy(k, sending, received, send_sem, recv_sem):
@@ -363,33 +375,42 @@
     )
 
 
+def in_plane(n):
+    z, core, j = place()
+    return 2 * (n // 4) + core, (n % 4) * 4 + j % 4
+
+
 def plane_copy(src, dst, sems, d):
     z, core, j = place()
     return pltpu.make_async_remote_copy(
         src_ref=src, dst_ref=dst, send_sem=sems.at[0, d], recv_sem=sems.at[1, d],
-        device_id=(2 * z + core, (j + d) % 16), device_id_type=MESH,
+        device_id=in_plane((z * 4 + j // 4 + d) % 16), device_id_type=MESH,
     )
 
 
+def in_column(d):
+    z, core, j = place()
+    return 2 * z + core, j // 4 * 4 + (j + d) % 4
+
+
 def column_copy(src, dst, sems, d):
-    z, core, j = place()
     return pltpu.make_async_remote_copy(
         src_ref=src, dst_ref=dst, send_sem=sems.at[0, d], recv_sem=sems.at[1, d],
-        device_id=(2 * ((z + d) % 4) + core, j), device_id_type=MESH,
+        device_id=in_column(d), device_id_type=MESH,
     )
 
 
 def greet_summers(barrier):
     z, core, j = place()
 
-    def greet(i, j):
-        pl.semaphore_signal(barrier, inc=1, device_id=(i, j), device_id_type=MESH)
-
-    greet(2 * z + 1 - core, j)
+    def greet(where):
+        pl.semaphore_signal(barrier, inc=1, device_id=where, device_id_type=MESH)
+
+    greet((2 * z + 1 - core, j))
     for d in range(1, 16):
-        greet(2 * z + core, (j + d) % 16)
+        greet(in_plane((z * 4 + j // 4 + d) % 16))
     for d in range(1, 4):
-        greet(2 * ((z + d) % 4) + core, j)
+        greet(in_column(d))
     return 19
 
 
@@ -405,7 +426,7 @@
 
 
 def kernel(
-    vol, cot, w, bias, lists, kmap, act, grad, weight_total, bias_total,
+    vol, cot, w, bias, lists, kmap, act, grad, total,
     nat, lin, x32, t32, wide, ct, faces, sending, received, x, g,
     a_planes, e_planes, c_planes, w2, wa, gt,
     d32, d16, from_sibling, h32, h16, from_plane, column, share, gathered, whole,
@@ -414,35 +435,39 @@
     halo = (sending, received, send_sem, recv_sem)
     planes = (a_planes, e_planes, c_planes)
     z, core, j = place()
+    n = z * 4 + j // 4
     take_vol = pltpu.make_async_copy(vol, nat, own_sems.at[0])
     take_cot = pltpu.make_async_copy(cot, nat, own_sems.at[1])
     give_act = pltpu.make_async_copy(nat, act, own_sems.at[2])
     give_grad = pltpu.make_async_copy(nat, grad, own_sems.at[3])
+    give_total = pltpu.make_async_copy(whole, total, own_sems.at[4])
     take_vol.start()
     barrier = pltpu.get_barrier_semaphore()
     neighbours = greet_neighbours(barrier)
     summers = greet_summers(barrier)
 
-    def put_x(a, e, c, v):
-        x32[pl.ds(rows16((1 + a) * SP + (1 + e) * SQ + (1 + c) * SR), 16)] = v
-        x[1 + a, 1 + e, 1 + c] = v.astype(BF16)
-
     take_vol.wait()
-    natural_to_bricks(nat, lin, put_x)
+    natural_to_bricks(nat, x32)
     take_cot.start()
     own_table(x32, t32, faces)
     pack_lists(lists, faces, sending)
     pl.semaphore_wait(barrier, neighbours + summers)
     start_halo(*halo)
 
+    def put_x(a, e, c, v):
+        x[1 + a, 1 + e, 1 + c] = v
+
+    each_inner(x32, put_x)
+
     def put_cot(a, e, c, v):
-        ct[pl.ds(rows16((a * 64 + e * 8 + c) * 16), 16)] = v.astype(BF16)
+        ct[pl.ds(rows16((a * 64 + e * 8 + c) * 16), 16)] = v
 
     take_cot.wait()
-    natural_to_bricks(nat, lin, put_cot)
+    natural_to_bricks(nat, x32)
+    each_inner(x32, put_cot)
     wide_weights(w, w2, wa, False)
     clear_rims(planes, x, g)
-    inner_conv(x, w2, lin, 0, 4)
+    inner_conv(x, w2, wa, lin, 0, 4)
     wait_halo(*halo)
     received_table(received, t32, wide)
     credit_neighbours(credit)
@@ -451,14 +476,15 @@
 
     def finish(ae, _):
         a, e = ae // 8, ae % 8
-        rows = pl.ds(rows16(ae * 128), 128)
-        linear = lin[rows] + bias[...]
+        line = pl.multiple_of(ae * LINE, 8)
+        linear = lin[pl.ds(line, 128)] + bias[...]
         s = 1.0 / (1.0 + jnp.exp(-linear))
         activated = linear * s
-        slope = ct[rows].astype(F32) * s * (1.0 + linear * (1.0 - s))
+        slope = ct[pl.ds(rows16(ae * 128), 128)].astype(F32) * s * (1.0 + linear * (1.0 - s))
         for c in range(8):
-            lin[pl.ds(ae * 128 + c, 16, stride=8)] = activated[c * 16 : c * 16 + 16]
-        x32[pl.ds(rows16((1 + a) * SP + (1 + e) * SQ + SR), 128)] = slope
+            lin[pl.ds(line + c * 17, 16)] = activated[c * 16 : c * 16 + 16]
+            at = (1 + a) * SP + (1 + e) * SQ + (1 + c) * SR
+            x32[pl.ds(at, 16)] = slope[c * 16 : c * 16 + 16]
         g[1 + a, 1 + e, 1:9] = slope.astype(BF16).reshape(8, 16, CH)
         return 0
 
@@ -472,10 +498,10 @@
     bricks_to_natural(lin, nat)
     give_act.start()
 
-    def turn(n, sums):
+    def turn(p, sums):
         for m in range(8):
-            block = g[1 + n, 1 + m, 1:9].astype(F32).reshape(128, CH)
-            gt[n // 2, pl.ds(rows16((n % 2) * CH), CH), m * 128 : m * 128 + 128] = (
+            block = g[1 + p, 1 + m, 1:9].astype(F32).reshape(128, CH)
+            gt[p // 2, pl.ds(rows16((p % 2) * CH), CH), m * 128 : m * 128 + 128] = (
                 block.T.astype(BF16)
             )
             sums = sums + block
@@ -486,72 +512,72 @@
         [jnp.sum(sums, axis=0, keepdims=True), jnp.zeros((127, CH), F32)], axis=0
     )
 
-    def tap(t, _):
-        e, c = t // 3, t % 3
-        parts = [
-            jnp.concatenate(
-                [x[2 * i + k, pl.ds(e, 8), pl.ds(c, 8)].reshape(1024, CH) for i in range(4)],
-                axis=0,
+    slopes = jnp.concatenate([gt[i] for i in range(4)], axis=1)
+    for e in range(3):
+        for c in range(3):
+            parts = [
+                jnp.concatenate(
+                    [x[2 * i + k, e : e + 8, c : c + 8].reshape(1024, CH) for i in range(4)],
+                    axis=0,
+                )
+                for k in range(4)
+            ]
+            terms = jnp.dot(
+                slopes, jnp.concatenate(parts, axis=1), preferred_element_type=F32
             )
-            for k in range(4)
-        ]
-        terms = jnp.dot(
-            jnp.concatenate([gt[i] for i in range(4)], axis=1),
-            jnp.concatenate(parts, axis=1),
-            preferred_element_type=F32,
-        )
-        for a in range(3):
-            term = (
-                terms[:CH, a * CH : (a + 1) * CH] + terms[CH:, (a + 1) * CH : (a + 2) * CH]
-            )
-            d32[pl.ds(rows16((a * 9 + t) * CH), CH)] = term.T
-        return 0
-
-    lax.fori_loop(0, 9, tap, 0)
+            for a in range(3):
+                term = (
+                    terms[:CH, a * CH : (a + 1) * CH]
+                    + terms[CH:, (a + 1) * CH : (a + 2) * CH]
+                )
+                at = (a * 9 + e * 3 + c) * CH
+                d32[at : at + CH] = term.T
+
     mine = pl.ds(rows16(core * HALF), HALF)
     other = pl.ds(rows16((1 - core) * HALF), HALF)
     d16[...] = d32[other].astype(BF16)
     sibling_copy(d16, from_sibling, sib_sems, 0).start()
     wide_weights(w, w2, wa, True)
-    inner_conv(g, w2, lin, 0, 1)
+    inner_conv(g, w2, wa, lin, 0, 1)
 
     sibling_copy(d16, from_sibling, sib_sems, 0).wait()
     h32[...] = d32[mine] + from_sibling[...].astype(F32)
     h16[...] = h32[...].astype(BF16).reshape(16, SHARE, CH)
     for d in range(1, 16):
-        plane_copy(h16.at[(j + d) % 16], from_plane.at[d - 1], out_sems, d).start()
-    inner_conv(g, w2, lin, 1, 4)
+        plane_copy(h16.at[(n + d) % 16], from_plane.at[d - 1], out_sems, d).start()
+    inner_conv(g, w2, wa, lin, 1, 4)
     for d in range(1, 16):
-        plane_copy(h16.at[(j + d) % 16], from_plane.at[d - 1], out_sems, d).wait()
-    part = h32[pl.ds(rows16(j * SHARE), SHARE)]
+        plane_copy(h16.at[(n + d) % 16], from_plane.at[d - 1], out_sems, d).wait()
+    part = h32[pl.ds(rows16(n * SHARE), SHARE)]
     for d in range(1, 16):
         part = part + from_plane[d - 1].astype(F32)
-    column[z] = part.astype(BF16)
+    column[j % 4] = part.astype(BF16)
     for d in range(1, 4):
-        column_copy(column.at[z], column.at[z], col_sems, d).start()
+        column_copy(column.at[j % 4], column.at[j % 4], col_sems, d).start()
     wait_halo(*halo)
     received_table(received, t32, wide)
     for d in range(1, 4):
-        column_copy(column.at[z], column.at[z], col_sems, d).wait()
+        column_copy(column.at[j % 4], column.at[j % 4], col_sems, d).wait()
     part = column[0].astype(F32)
-    for n in range(1, 4):
-        part = part + column[n].astype(F32)
+    for m in range(1, 4):
+        part = part + column[m].astype(F32)
     voxels = lax.axis_size("gx") * lax.axis_size("gy") * 8192
     share[...] = (part * (1.0 / math.sqrt(voxels))).astype(BF16)
-    gathered[j] = share[...]
+    gathered[n] = share[...]
     for d in range(1, 16):
-        plane_copy(share, gathered.at[j], in_sems, d).start()
+        plane_copy(share, gathered.at[n], in_sems, d).start()
     rim(kmap, t32, x32, planes, None)
     for d in range(1, 16):
-        plane_copy(share, gathered.at[j], in_sems, d).wait()
+        plane_copy(share, gathered.at[n], in_sems, d).wait()
     sibling_copy(gathered, whole.at[core], sib_sems, 1).start()
     whole[core] = gathered[...]
     rim_conv(planes, w2, wa, lin)
 
     def settle(ae, _):
-        block = lin[pl.ds(rows16(ae * 128), 128)]
-        for c in range(8):
-            lin[pl.ds(ae * 128 + c, 16, stride=8)] = block[c * 16 : c * 16 + 16]
+        line = pl.multiple_of(ae * LINE, 8)
+        block = lin[pl.ds(line, 128)]
+        for c in range(1, 8):
+            lin[pl.ds(line + c * 17, 16)] = block[c * 16 : c * 16 + 16]
         return 0
 
     lax.fori_loop(0, 64, settle, 0)
@@ -559,11 +585,9 @@
     bricks_to_natural(lin, nat)
     give_grad.start()
     sibling_copy(gathered, whole.at[core], sib_sems, 1).wait()
-    weight_total[0:HALF] = whole[0].reshape(HALF, CH).astype(F32)
-    last = whole[1].reshape(HALF, CH).astype(F32)
-    weight_total[HALF:] = last[: 27 * CH - HALF]
-    bias_total[...] = last[27 * CH - HALF : 27 * CH - HALF + 8]
+    give_total.start()
     wait_halo_sent(*halo)
+    give_total.wait()
     give_grad.wait()
 
 
@@ -578,15 +602,14 @@
         out_shape=(
             jax.ShapeDtypeStruct((16, 512, CH), BF16),
             jax.ShapeDtypeStruct((16, 512, CH), BF16),
-            jax.ShapeDtypeStruct((27 * CH, CH), F32),
-            jax.ShapeDtypeStruct((8, CH), F32),
+            jax.ShapeDtypeStruct((2, 16, SHARE, CH), BF16),
         ),
         in_specs=[hbm, hbm, vm, vm, sm, sm],
-        out_specs=(hbm, hbm, vm, vm),
+        out_specs=(hbm, hbm, hbm),
         scratch_shapes=[
             pltpu.VMEM((16, 512, CH), BF16),
-            pltpu.VMEM((8192, CH), F32),
-            pltpu.VMEM((16000, CH), F32),
+            pltpu.VMEM((64 * LINE, CH), F32),
+            pltpu.VMEM((10 * SP + 2, CH), F32),
             pltpu.VMEM((49 * ENTRY, 8, CH), F32),
             pltpu.VMEM((256, CH), F32),
             pltpu.VMEM((8192, CH), BF16),
@@ -617,7 +640,7 @@
             pltpu.SemaphoreType.DMA((2, 16)),
             pltpu.SemaphoreType.DMA((2, 4)),
             pltpu.SemaphoreType.DMA((2, 16)),
-            pltpu.SemaphoreType.DMA((4,)),
+            pltpu.SemaphoreType.DMA((5,)),
             pltpu.SemaphoreType.REGULAR,
         ],
         compiler_params=pltpu.CompilerParams(
@@ -627,20 +650,61 @@
     )(vol, cot, w, bias, lists, kmap)
 
 
+PIECES = 4
+
+
+def deliver_kernel(act, grad, total, act_out, grad_out, weight_out, bias_out, sems):
+    copies = [
+        pltpu.make_async_copy(
+            src.at[pl.ds(m * 16 // PIECES, 16 // PIECES)],
+            dst.at[pl.ds(m * 16 // PIECES, 16 // PIECES)],
+            sems.at[n, m],
+        )
+        for n, (src, dst) in enumerate(((act, act_out), (grad, grad_out)))
+        for m in range(PIECES)
+    ]
+    for copy in copies:
+        copy.start()
+    weight_out[...] = total[: 27 * CH].astype(F32)
+    bias_out[...] = total[27 * CH : 27 * CH + 16].astype(F32)[0:1]
+    for copy in copies:
+        copy.wait()
+
+
+def deliver(act, grad, total):
+    vm = pl.BlockSpec(memory_space=pltpu.VMEM)
+    hbm = pl.BlockSpec(memory_space=pl.ANY)
+    return pl.pallas_call(
+        deliver_kernel,
+        out_shape=(
+            jax.ShapeDtypeStruct(act.shape, BF16),
+            jax.ShapeDtypeStruct(grad.shape, BF16),
+            jax.ShapeDtypeStruct((27 * CH, CH), F32),
+            jax.ShapeDtypeStruct((1, CH), F32),
+        ),
+        in_specs=[hbm, hbm, vm],
+        out_specs=(hbm, hbm, vm, vm),
+        scratch_shapes=[pltpu.SemaphoreType.DMA((2, PIECES))],
+        compiler_params=pltpu.CompilerParams(vmem_limit_bytes=63 * 2**20),
+        name="deliver",
+    )(act, grad, total)
+
+
 def shards(features, cotangent, kernel_weight, conv_bias, send_lists, kernel_map):
-    act, grad, weight_total, bias_total = layer(
+    act, grad, total = layer(
         features.reshape(16, 512, CH),
         cotangent.reshape(16, 512, CH),
         kernel_weight.reshape(27, CH, CH),
         conv_bias.reshape(1, CH),
-        send_lists[0, 0],
+        send_lists[0, 0].T,
         kernel_map[0, 0],
     )
+    act, grad, weight_total, bias_total = deliver(act, grad, total.reshape(ROWS, CH))
     return (
         act.reshape(features.shape),
         grad.reshape(features.shape),
         weight_total.reshape(kernel_weight.shape),
-        bias_total[0],
+        bias_total.reshape(CH),
     )
 
 

time: 106 us -> 217 us (2.05)
  the two profiles are of different devices: /device:TPU:0 before, /device:TPU:1 now
where the time goes in v3:
time: 217 us; the launch traced here: 216 us
  Pallas kernels  215 us (99%)
    pallas_call x1, Pallas kernels, deliver(): pl.pallas_call(deliver_kernel, out_shape=(jax.ShapeDtypeStruct(act.shape,...  131 us
    pallas_call x1, Pallas kernels, layer(): pl.pallas_call(kernel, out_shape=(jax.ShapeDtypeStruct((16, 512, CH), BF1...  84.2 us

profile of v3, /device:TPU:1, one launch (start us, length us, event | category | flops | bytes accessed | tf_op | source)
XLA Modules:
  0.0 215.6 jit_solution(14676834771255195747)
XLA Ops:
  0.6 84.2 %layer.1 = (bf16[16,512,128]{2,1,0:T(8,128)(2,1)}, bf16[16,512,128]{2,1,0:T(8,128)(2,1)}, bf16[2,16,112,128]{3,2,1,0:T(8,128)(2,1)}) custom-call(bf16[16,512,128]{2,1,0:T(8,128)(2,1)} %bitcast.13, bf16[16,512,128]{2,1,0:T(8,128)(2,1)} %bitcast.14, bf16[27,128,128]{2,1,0:T(8,128)(2,1)} %bitcast.16, f32[1,128]{1,0:T(1,128)} %bitcast.19, s32[4,8]{1,0:T(4,128)} %bitcast.18, ...), custom_call_target="tpu_custom_call" | custom-call | tf_op jit(solution)/shard_map/layer/pallas_call | solution.py:600
  84.8 130.6 %deliver.1 = (bf16[16,512,128]{2,1,0:T(8,128)(2,1)}, bf16[16,512,128]{2,1,0:T(8,128)(2,1)}, f32[3456,128]{1,0:T(8,128)}, f32[1,128]{1,0:T(1,128)}) custom-call(bf16[16,512,128]{2,1,0:T(8,128)(2,1)} %get-tuple-element.11.act, bf16[16,512,128]{2,1,0:T(8,128)(2,1)} %get-tuple-element.12.grad, bf16[3584,128]{1,0:T(8,128)(2,1)} %bitcast.15), custom_call_target="tpu_custom_call" | custom-call | tf_op jit(solution)/shard_map/deliver/pallas_call | solution.py:677

commit v4 on v3

--- a/solution.py
+++ b/solution.py
@@ -357,9 +357,8 @@
             halo_copy(k, *halo).wait_send()
 
 
-ROWS = 3584
-HALF = ROWS // 2
-SHARE = HALF // 16
+ROWS = 28 * CH
+PARTS = ((0, 16), (16, 12))
 
 
 def place():
@@ -414,6 +413,99 @@
     return 19
 
 
+class Summed:
+    def __init__(self, d32, first, refs):
+        self.d32, self.first = d32, first
+        (
+            self.d16, self.from_sibling, self.h32, self.h16, self.from_plane, self.column,
+            self.share, self.gathered, self.whole, self.sib, self.out, self.col, self.back,
+        ) = refs
+        self.half = self.d16.shape[0]
+        self.rows = self.share.shape[0]
+        z, self.core, j = place()
+        self.n, self.y = z * 4 + j // 4, j % 4
+
+    def first_pair(self):
+        return sibling_copy(self.d16, self.from_sibling, self.sib, 0)
+
+    def outward(self, d):
+        there = (self.n + d) % 16
+        return plane_copy(self.h16.at[there], self.from_plane.at[d - 1], self.out, d)
+
+    def upward(self, d):
+        return column_copy(self.column.at[self.y], self.column.at[self.y], self.col, d)
+
+    def inward(self, d):
+        return plane_copy(self.share, self.gathered.at[self.n], self.back, d)
+
+    def last_pair(self):
+        return sibling_copy(self.gathered, self.whole.at[self.core], self.sib, 1)
+
+    def start_pair(self):
+        other = pl.ds(rows16(self.first + (1 - self.core) * self.half), self.half)
+        self.d16[...] = self.d32[other].astype(BF16)
+        self.first_pair().start()
+
+    def start_plane(self):
+        self.first_pair().wait()
+        mine = pl.ds(rows16(self.first + self.core * self.half), self.half)
+        self.h32[...] = self.d32[mine] + self.from_sibling[...].astype(F32)
+        self.h16[...] = self.h32[...].astype(BF16).reshape(self.h16.shape)
+        for d in range(1, 16):
+            self.outward(d).start()
+
+    def start_column(self):
+        for d in range(1, 16):
+            self.outward(d).wait()
+        part = self.h32[pl.ds(rows16(self.n * self.rows), self.rows)]
+        for d in range(1, 16):
+            part = part + self.from_plane[d - 1].astype(F32)
+        self.column[self.y] = part.astype(BF16)
+        for d in range(1, 4):
+            self.upward(d).start()
+
+    def start_back(self):
+        for d in range(1, 4):
+            self.upward(d).wait()
+        part = self.column[0].astype(F32)
+        for m in range(1, 4):
+            part = part + self.column[m].astype(F32)
+        voxels = lax.axis_size("gx") * lax.axis_size("gy") * 8192
+        self.share[...] = (part * (1.0 / math.sqrt(voxels))).astype(BF16)
+        self.gathered[self.n] = self.share[...]
+        for d in range(1, 16):
+            self.inward(d).start()
+
+    def start_last(self):
+        for d in range(1, 16):
+            self.inward(d).wait()
+        self.last_pair().start()
+        self.whole[self.core] = self.gathered[...]
+
+    def finish(self):
+        self.last_pair().wait()
+
+
+def sum_scratch(blocks):
+    half = blocks * CH // 2
+    rows = half // 16
+    return [
+        pltpu.VMEM((half, CH), BF16),
+        pltpu.VMEM((half, CH), BF16),
+        pltpu.VMEM((half, CH), F32),
+        pltpu.VMEM((16, rows, CH), BF16),
+        pltpu.VMEM((15, rows, CH), BF16),
+        pltpu.VMEM((4, rows, CH), BF16),
+        pltpu.VMEM((rows, CH), BF16),
+        pltpu.VMEM((16, rows, CH), BF16),
+        pltpu.VMEM((2, 16, rows, CH), BF16),
+        pltpu.SemaphoreType.DMA((2, 2)),
+        pltpu.SemaphoreType.DMA((2, 16)),
+        pltpu.SemaphoreType.DMA((2, 4)),
+        pltpu.SemaphoreType.DMA((2, 16)),
+    ]
+
+
 def credit_neighbours(credit):
     i, j = lax.axis_index("gx"), lax.axis_index("gy")
     for dx, dy in DIRECTIONS:
@@ -426,21 +518,20 @@
 
 
 def kernel(
-    vol, cot, w, bias, lists, kmap, act, grad, total,
+    vol, cot, w, bias, lists, kmap, act, grad, total_a, total_b,
     nat, lin, x32, t32, wide, ct, faces, sending, received, x, g,
-    a_planes, e_planes, c_planes, w2, wa, gt,
-    d32, d16, from_sibling, h32, h16, from_plane, column, share, gathered, whole,
-    send_sem, recv_sem, sib_sems, out_sems, col_sems, in_sems, own_sems, credit,
+    a_planes, e_planes, c_planes, w2, wa, gt, d32, send_sem, recv_sem, own_sems, credit, *sums,
 ):
     halo = (sending, received, send_sem, recv_sem)
     planes = (a_planes, e_planes, c_planes)
-    z, core, j = place()
-    n = z * 4 + j // 4
+    early = Summed(d32, PARTS[0][0] * CH, sums[: len(sums) // 2])
+    late = Summed(d32, PARTS[1][0] * CH, sums[len(sums) // 2 :])
     take_vol = pltpu.make_async_copy(vol, nat, own_sems.at[0])
     take_cot = pltpu.make_async_copy(cot, nat, own_sems.at[1])
     give_act = pltpu.make_async_copy(nat, act, own_sems.at[2])
     give_grad = pltpu.make_async_copy(nat, grad, own_sems.at[3])
-    give_total = pltpu.make_async_copy(whole, total, own_sems.at[4])
+    give_early = pltpu.make_async_copy(early.whole, total_a, own_sems.at[4])
+    give_late = pltpu.make_async_copy(late.whole, total_b, own_sems.at[5])
     take_vol.start()
     barrier = pltpu.get_barrier_semaphore()
     neighbours = greet_neighbours(barrier)
@@ -507,9 +598,9 @@
             sums = sums + block
         return sums
 
-    sums = lax.fori_loop(0, 8, turn, jnp.zeros((128, CH), F32))
+    totals = lax.fori_loop(0, 8, turn, jnp.zeros((128, CH), F32))
     d32[27 * CH :] = jnp.concatenate(
-        [jnp.sum(sums, axis=0, keepdims=True), jnp.zeros((127, CH), F32)], axis=0
+        [jnp.sum(totals, axis=0, keepdims=True), jnp.zeros((127, CH), F32)], axis=0
     )
 
     slopes = jnp.concatenate([gt[i] for i in range(4)], axis=1)
@@ -530,48 +621,28 @@
                     terms[:CH, a * CH : (a + 1) * CH]
                     + terms[CH:, (a + 1) * CH : (a + 2) * CH]
                 )
-                at = (a * 9 + e * 3 + c) * CH
+                at = (e * 9 + c * 3 + a) * CH
                 d32[at : at + CH] = term.T
-
-    mine = pl.ds(rows16(core * HALF), HALF)
-    other = pl.ds(rows16((1 - core) * HALF), HALF)
-    d16[...] = d32[other].astype(BF16)
-    sibling_copy(d16, from_sibling, sib_sems, 0).start()
+        if e == 1:
+            early.start_pair()
+
+    late.start_pair()
+    early.start_plane()
     wide_weights(w, w2, wa, True)
     inner_conv(g, w2, wa, lin, 0, 1)
-
-    sibling_copy(d16, from_sibling, sib_sems, 0).wait()
-    h32[...] = d32[mine] + from_sibling[...].astype(F32)
-    h16[...] = h32[...].astype(BF16).reshape(16, SHARE, CH)
-    for d in range(1, 16):
-        plane_copy(h16.at[(n + d) % 16], from_plane.at[d - 1], out_sems, d).start()
-    inner_conv(g, w2, wa, lin, 1, 4)
-    for d in range(1, 16):
-        plane_copy(h16.at[(n + d) % 16], from_plane.at[d - 1], out_sems, d).wait()
-    part = h32[pl.ds(rows16(n * SHARE), SHARE)]
-    for d in range(1, 16):
-        part = part + from_plane[d - 1].astype(F32)
-    column[j % 4] = part.astype(BF16)
-    for d in range(1, 4):
-        column_copy(column.at[j % 4], column.at[j % 4], col_sems, d).start()
+    late.start_plane()
+    inner_conv(g, w2, wa, lin, 1, 3)
+    early.start_column()
+    inner_conv(g, w2, wa, lin, 3, 4)
+    late.start_column()
+    early.start_back()
     wait_halo(*halo)
     received_table(received, t32, wide)
-    for d in range(1, 4):
-        column_copy(column.at[j % 4], column.at[j % 4], col_sems, d).wait()
-    part = column[0].astype(F32)
-    for m in range(1, 4):
-        part = part + column[m].astype(F32)
-    voxels = lax.axis_size("gx") * lax.axis_size("gy") * 8192
-    share[...] = (part * (1.0 / math.sqrt(voxels))).astype(BF16)
-    gathered[n] = share[...]
-    for d in range(1, 16):
-        plane_copy(share, gathered.at[n], in_sems, d).start()
+    late.start_back()
     rim(kmap, t32, x32, planes, None)
-    for d in range(1, 16):
-        plane_copy(share, gathered.at[n], in_sems, d).wait()
-    sibling_copy(gathered, whole.at[core], sib_sems, 1).start()
-    whole[core] = gathered[...]
+    early.start_last()
     rim_conv(planes, w2, wa, lin)
+    late.start_last()
 
     def settle(ae, _):
         line = pl.multiple_of(ae * LINE, 8)
@@ -584,10 +655,13 @@
     give_act.wait()
     bricks_to_natural(lin, nat)
     give_grad.start()
-    sibling_copy(gathered, whole.at[core], sib_sems, 1).wait()
-    give_total.start()
+    early.finish()
+    give_early.start()
+    late.finish()
+    give_late.start()
     wait_halo_sent(*halo)
-    give_total.wait()
+    give_early.wait()
+    give_late.wait()
     give_grad.wait()
 
 
@@ -602,10 +676,12 @@
         out_shape=(
             jax.ShapeDtypeStruct((16, 512, CH), BF16),
             jax.ShapeDtypeStruct((16, 512, CH), BF16),
-            jax.ShapeDtypeStruct((2, 16, SHARE, CH), BF16),
+            *[
+                jax.ShapeDtypeStruct((2, 16, blocks * 4, CH), BF16) for _, blocks in PARTS
+            ],
         ),
         in_specs=[hbm, hbm, vm, vm, sm, sm],
-        out_specs=(hbm, hbm, hbm),
+        out_specs=(hbm, hbm, hbm, hbm),
         scratch_shapes=[
             pltpu.VMEM((16, 512, CH), BF16),
             pltpu.VMEM((64 * LINE, CH), F32),
@@ -625,23 +701,11 @@
             pltpu.VMEM((2, 12 * CH, 2 * CH), BF16),
             pltpu.VMEM((4, 2 * CH, 1024), BF16),
             pltpu.VMEM((ROWS, CH), F32),
-            pltpu.VMEM((HALF, CH), BF16),
-            pltpu.VMEM((HALF, CH), BF16),
-            pltpu.VMEM((HALF, CH), F32),
-            pltpu.VMEM((16, SHARE, CH), BF16),
-            pltpu.VMEM((15, SHARE, CH), BF16),
-            pltpu.VMEM((4, SHARE, CH), BF16),
-            pltpu.VMEM((SHARE, CH), BF16),
-            pltpu.VMEM((16, SHARE, CH), BF16),
-            pltpu.VMEM((2, 16, SHARE, CH), BF16),
             pltpu.SemaphoreType.DMA((8,)),
             pltpu.SemaphoreType.DMA((8,)),
-            pltpu.SemaphoreType.DMA((2, 2)),
-            pltpu.SemaphoreType.DMA((2, 16)),
-            pltpu.SemaphoreType.DMA((2, 4)),
-            pltpu.SemaphoreType.DMA((2, 16)),
-            pltpu.SemaphoreType.DMA((5,)),
+            pltpu.SemaphoreType.DMA((6,)),
             pltpu.SemaphoreType.REGULAR,
+            *[ref for _, blocks in PARTS for ref in sum_scratch(blocks)],
         ],
         compiler_params=pltpu.CompilerParams(
             collective_id=0, has_side_effects=True, vmem_limit_bytes=63 * 2**20
@@ -653,25 +717,35 @@
 PIECES = 4
 
 
-def deliver_kernel(act, grad, total, act_out, grad_out, weight_out, bias_out, sems):
-    copies = [
-        pltpu.make_async_copy(
-            src.at[pl.ds(m * 16 // PIECES, 16 // PIECES)],
-            dst.at[pl.ds(m * 16 // PIECES, 16 // PIECES)],
-            sems.at[n, m],
+def deliver_kernel(act, grad, total_a, total_b, act_out, grad_out, weight_out, bias_out, held, sems):
+    def piece(n, m, src, dst):
+        at = pl.ds(m * 16 // PIECES, 16 // PIECES)
+        return (
+            pltpu.make_async_copy(src.at[at], held.at[n, at], sems.at[0, n, m]),
+            pltpu.make_async_copy(held.at[n, at], dst.at[at], sems.at[1, n, m]),
         )
+
+    pieces = [
+        piece(n, m, src, dst)
         for n, (src, dst) in enumerate(((act, act_out), (grad, grad_out)))
         for m in range(PIECES)
     ]
-    for copy in copies:
-        copy.start()
-    weight_out[...] = total[: 27 * CH].astype(F32)
-    bias_out[...] = total[27 * CH : 27 * CH + 16].astype(F32)[0:1]
-    for copy in copies:
-        copy.wait()
-
-
-def deliver(act, grad, total):
+    for take, _ in pieces:
+        take.start()
+    for take, give in pieces:
+        take.wait()
+        give.start()
+    for n in range(28):
+        total, at = (total_a, n * CH) if n < PARTS[1][0] else (total_b, (n - PARTS[1][0]) * CH)
+        if n < 27:
+            weight_out[n % 3 * 9 + n // 3] = total[at : at + CH].astype(F32)
+        else:
+            bias_out[...] = total[at : at + 16].astype(F32)[0:1]
+    for _, give in pieces:
+        give.wait()
+
+
+def deliver(act, grad, total_a, total_b):
     vm = pl.BlockSpec(memory_space=pltpu.VMEM)
     hbm = pl.BlockSpec(memory_space=pl.ANY)
     return pl.pallas_call(
@@ -679,19 +753,22 @@
         out_shape=(
             jax.ShapeDtypeStruct(act.shape, BF16),
             jax.ShapeDtypeStruct(grad.shape, BF16),
-            jax.ShapeDtypeStruct((27 * CH, CH), F32),
+            jax.ShapeDtypeStruct((27, CH, CH), F32),
             jax.ShapeDtypeStruct((1, CH), F32),
         ),
-        in_specs=[hbm, hbm, vm],
+        in_specs=[hbm, hbm, vm, vm],
         out_specs=(hbm, hbm, vm, vm),
-        scratch_shapes=[pltpu.SemaphoreType.DMA((2, PIECES))],
+        scratch_shapes=[
+            pltpu.VMEM((2, 16, 512, CH), BF16),
+            pltpu.SemaphoreType.DMA((2, 2, PIECES)),
+        ],
         compiler_params=pltpu.CompilerParams(vmem_limit_bytes=63 * 2**20),
         name="deliver",
-    )(act, grad, total)
+    )(act, grad, total_a, total_b)
 
 
 def shards(features, cotangent, kernel_weight, conv_bias, send_lists, kernel_map):
-    act, grad, total = layer(
+    act, grad, total_a, total_b = layer(
         features.reshape(16, 512, CH),
         cotangent.reshape(16, 512, CH),
         kernel_weight.reshape(27, CH, CH),
@@ -699,7 +776,9 @@
         send_lists[0, 0].T,
         kernel_map[0, 0],
     )
-    act, grad, weight_total, bias_total = deliver(act, grad, total.reshape(ROWS, CH))
+    act, grad, weight_total, bias_total = deliver(
+        act, grad, total_a.reshape(-1, CH), total_b.reshape(-1, CH)
+    )
     return (
         act.reshape(features.shape),
         grad.reshape(features.shape),

time: 217 us -> 93.1 us (0.43)
  Pallas kernels: 215 us -> 92 us
    pallas_call x1, Pallas kernels: 131 us -> 5.94 us  [deliver(): pl.pallas_call(deliver_kernel, out_shape=(jax.ShapeDtypeStruct(act.shape,...]
where the time goes in v4:
time: 93.1 us; the launch traced here: 92.9 us
  Pallas kernels  92 us (99%)
    pallas_call x1, Pallas kernels, layer(): pl.pallas_call(kernel, out_shape=(jax.ShapeDtypeStruct((16, 512, CH), BF1...  86.1 us
    pallas_call x1, Pallas kernels, deliver(): pl.pallas_call(deliver_kernel, out_shape=(jax.ShapeDtypeStruct(act.shape,...  5.94 us

profile of v4, /device:TPU:1, one launch (start us, length us, event | category | flops | bytes accessed | tf_op | source)
XLA Modules:
  0.0 92.9 jit_solution(15716550185753129535)
XLA Ops:
  0.6 86.1 %layer.1 = (bf16[16,512,128]{2,1,0:T(8,128)(2,1)}, bf16[16,512,128]{2,1,0:T(8,128)(2,1)}, bf16[2,16,64,128]{3,2,1,0:T(8,128)(2,1)}, bf16[2,16,48,128]{3,2,1,0:T(8,128)(2,1)}) custom-call(bf16[16,512,128]{2,1,0:T(8,128)(2,1)} %bitcast.14, bf16[16,512,128]{2,1,0:T(8,128)(2,1)} %bitcast.15, bf16[27,128,128]{2,1,0:T(8,128)(2,1)} %bitcast.16, f32[1,128]{1,0:T(1,128)} %bitcast.21, ...), custom_call_target="tpu_custom_call" | custom-call | tf_op jit(solution)/shard_map/layer/pallas_call | solution.py:674
  86.7 5.9 %deliver.1 = (bf16[16,512,128]{2,1,0:T(8,128)(2,1)}, bf16[16,512,128]{2,1,0:T(8,128)(2,1)}, f32[27,128,128]{2,1,0:T(8,128)}, f32[1,128]{1,0:T(1,128)}) custom-call(bf16[16,512,128]{2,1,0:T(8,128)(2,1)} %get-tuple-element.12.act, bf16[16,512,128]{2,1,0:T(8,128)(2,1)} %get-tuple-element.13.grad, bf16[2048,128]{1,0:T(8,128)(2,1)} %bitcast.17, ...), custom_call_target="tpu_custom_call" | custom-call | tf_op jit(solution)/shard_map/deliver/pallas_call | solution.py:751

commit v5 on v4

--- a/solution.py
+++ b/solution.py
@@ -357,8 +357,8 @@
             halo_copy(k, *halo).wait_send()
 
 
-ROWS = 28 * CH
-PARTS = ((0, 16), (16, 12))
+BLOCKS = 28
+ROWS = BLOCKS * CH
 
 
 def place():
@@ -411,6 +411,75 @@
     for d in range(1, 4):
         greet(in_column(d))
     return 19
+
+
+def settle(lin):
+    def line(ae, _):
+        at = pl.multiple_of(ae * LINE, 8)
+        block = lin[pl.ds(at, 128)]
+        for c in range(1, 8):
+            lin[pl.ds(at + c * 17, 16)] = block[c * 16 : c * 16 + 16]
+        return 0
+
+    lax.fori_loop(0, 64, line, 0)
+
+
+def weight_terms(x, gt, d32):
+    def block(e, c, a):
+        at = (e * 9 + c * 3 + a) * CH
+        return slice(at, at + CH)
+
+    for j in range(2):
+        pairs = jnp.concatenate(
+            [
+                jnp.concatenate(
+                    [
+                        gt[i, j * CH : (j + 1) * CH, (2 * m + n) * CH : (2 * m + n + 1) * CH]
+                        for i in range(4)
+                        for m in range(4)
+                    ],
+                    axis=1,
+                )
+                for n in range(2)
+            ],
+            axis=0,
+        )
+        for c in range(3):
+            parts = [
+                jnp.concatenate(
+                    [
+                        x[2 * i + 3 * j]
+                        .reshape(5, 2, 10, 16, CH)[k // 2 : k // 2 + 4, k % 2, c : c + 8]
+                        .reshape(512, CH)
+                        for i in range(4)
+                    ],
+                    axis=0,
+                )
+                for k in range(4)
+            ]
+            terms = jnp.dot(pairs, jnp.concatenate(parts, axis=1), preferred_element_type=F32)
+            for e in range(3):
+                term = (
+                    terms[:CH, e * CH : (e + 1) * CH]
+                    + terms[CH:, (e + 1) * CH : (e + 2) * CH]
+                )
+                d32[block(e, c, 2 * j)] = term.T
+    slopes = jnp.concatenate([gt[i] for i in range(4)], axis=1)
+    for e in range(3):
+        for c in range(3):
+            parts = [
+                jnp.concatenate(
+                    [x[2 * i + k, e : e + 8, c : c + 8].reshape(1024, CH) for i in range(4)],
+                    axis=0,
+                )
+                for k in (1, 2)
+            ]
+            terms = jnp.dot(
+                slopes, jnp.concatenate(parts, axis=1), preferred_element_type=F32
+            )
+            d32[block(e, c, 0)] += terms[CH:, :CH].T
+            d32[block(e, c, 1)] = (terms[:CH, :CH] + terms[CH:, CH:]).T
+            d32[block(e, c, 2)] += terms[:CH, CH:].T
 
 
 class Summed:
@@ -518,20 +587,18 @@
 
 
 def kernel(
-    vol, cot, w, bias, lists, kmap, act, grad, total_a, total_b,
+    vol, cot, w, bias, lists, kmap, act, grad, total,
     nat, lin, x32, t32, wide, ct, faces, sending, received, x, g,
     a_planes, e_planes, c_planes, w2, wa, gt, d32, send_sem, recv_sem, own_sems, credit, *sums,
 ):
     halo = (sending, received, send_sem, recv_sem)
     planes = (a_planes, e_planes, c_planes)
-    early = Summed(d32, PARTS[0][0] * CH, sums[: len(sums) // 2])
-    late = Summed(d32, PARTS[1][0] * CH, sums[len(sums) // 2 :])
+    terms_sum = Summed(d32, 0, sums)
     take_vol = pltpu.make_async_copy(vol, nat, own_sems.at[0])
     take_cot = pltpu.make_async_copy(cot, nat, own_sems.at[1])
     give_act = pltpu.make_async_copy(nat, act, own_sems.at[2])
     give_grad = pltpu.make_async_copy(nat, grad, own_sems.at[3])
-    give_early = pltpu.make_async_copy(early.whole, total_a, own_sems.at[4])
-    give_late = pltpu.make_async_copy(late.whole, total_b, own_sems.at[5])
+    give_total = pltpu.make_async_copy(terms_sum.whole, total, own_sems.at[4])
     take_vol.start()
     barrier = pltpu.get_barrier_semaphore()
     neighbours = greet_neighbours(barrier)
@@ -572,8 +639,8 @@
         s = 1.0 / (1.0 + jnp.exp(-linear))
         activated = linear * s
         slope = ct[pl.ds(rows16(ae * 128), 128)].astype(F32) * s * (1.0 + linear * (1.0 - s))
+        lin[pl.ds(line, 128)] = activated
         for c in range(8):
-            lin[pl.ds(line + c * 17, 16)] = activated[c * 16 : c * 16 + 16]
             at = (1 + a) * SP + (1 + e) * SQ + (1 + c) * SR
             x32[pl.ds(at, 16)] = slope[c * 16 : c * 16 + 16]
         g[1 + a, 1 + e, 1:9] = slope.astype(BF16).reshape(8, 16, CH)
@@ -585,9 +652,6 @@
     pack_lists(lists, faces, sending)
     pl.semaphore_wait(credit, neighbours)
     start_halo(*halo)
-
-    bricks_to_natural(lin, nat)
-    give_act.start()
 
     def turn(p, sums):
         for m in range(8):
@@ -603,65 +667,30 @@
         [jnp.sum(totals, axis=0, keepdims=True), jnp.zeros((127, CH), F32)], axis=0
     )
 
-    slopes = jnp.concatenate([gt[i] for i in range(4)], axis=1)
-    for e in range(3):
-        for c in range(3):
-            parts = [
-                jnp.concatenate(
-                    [x[2 * i + k, e : e + 8, c : c + 8].reshape(1024, CH) for i in range(4)],
-                    axis=0,
-                )
-                for k in range(4)
-            ]
-            terms = jnp.dot(
-                slopes, jnp.concatenate(parts, axis=1), preferred_element_type=F32
-            )
-            for a in range(3):
-                term = (
-                    terms[:CH, a * CH : (a + 1) * CH]
-                    + terms[CH:, (a + 1) * CH : (a + 2) * CH]
-                )
-                at = (e * 9 + c * 3 + a) * CH
-                d32[at : at + CH] = term.T
-        if e == 1:
-            early.start_pair()
-
-    late.start_pair()
-    early.start_plane()
+    weight_terms(x, gt, d32)
+    terms_sum.start_pair()
+    settle(lin)
+    bricks_to_natural(lin, nat)
+    give_act.start()
     wide_weights(w, w2, wa, True)
-    inner_conv(g, w2, wa, lin, 0, 1)
-    late.start_plane()
-    inner_conv(g, w2, wa, lin, 1, 3)
-    early.start_column()
+    terms_sum.start_plane()
+    inner_conv(g, w2, wa, lin, 0, 3)
+    terms_sum.start_column()
     inner_conv(g, w2, wa, lin, 3, 4)
-    late.start_column()
-    early.start_back()
+    terms_sum.start_back()
     wait_halo(*halo)
     received_table(received, t32, wide)
-    late.start_back()
     rim(kmap, t32, x32, planes, None)
-    early.start_last()
     rim_conv(planes, w2, wa, lin)
-    late.start_last()
-
-    def settle(ae, _):
-        line = pl.multiple_of(ae * LINE, 8)
-        block = lin[pl.ds(line, 128)]
-        for c in range(1, 8):
-            lin[pl.ds(line + c * 17, 16)] = block[c * 16 : c * 16 + 16]
-        return 0
-
-    lax.fori_loop(0, 64, settle, 0)
+    terms_sum.start_last()
+    settle(lin)
     give_act.wait()
     bricks_to_natural(lin, nat)
     give_grad.start()
-    early.finish()
-    give_early.start()
-    late.finish()
-    give_late.start()
+    terms_sum.finish()
+    give_total.start()
     wait_halo_sent(*halo)
-    give_early.wait()
-    give_late.wait()
+    give_total.wait()
     give_grad.wait()
 
 
@@ -676,12 +705,10 @@
         out_shape=(
             jax.ShapeDtypeStruct((16, 512, CH), BF16),
             jax.ShapeDtypeStruct((16, 512, CH), BF16),
-            *[
-                jax.ShapeDtypeStruct((2, 16, blocks * 4, CH), BF16) for _, blocks in PARTS
-            ],
+            jax.ShapeDtypeStruct((2, 16, BLOCKS * 4, CH), BF16),
         ),
         in_specs=[hbm, hbm, vm, vm, sm, sm],
-        out_specs=(hbm, hbm, hbm, hbm),
+        out_specs=(hbm, hbm, hbm),
         scratch_shapes=[
             pltpu.VMEM((16, 512, CH), BF16),
             pltpu.VMEM((64 * LINE, CH), F32),
@@ -703,9 +730,9 @@
             pltpu.VMEM((ROWS, CH), F32),
             pltpu.SemaphoreType.DMA((8,)),
             pltpu.SemaphoreType.DMA((8,)),
-            pltpu.SemaphoreType.DMA((6,)),
+            pltpu.SemaphoreType.DMA((5,)),
             pltpu.SemaphoreType.REGULAR,
-            *[ref for _, blocks in PARTS for ref in sum_scratch(blocks)],
+            *sum_scratch(BLOCKS),
         ],
         compiler_params=pltpu.CompilerParams(
             collective_id=0, has_side_effects=True, vmem_limit_bytes=63 * 2**20
@@ -717,7 +744,9 @@
 PIECES = 4
 
 
-def deliver_kernel(act, grad, total_a, total_b, act_out, grad_out, weight_out, bias_out, held, sems):
+def deliver_kernel(
+    act, grad, total, act_out, grad_out, weight_out, bias_out, held, terms, weights, sems, more
+):
     def piece(n, m, src, dst):
         at = pl.ds(m * 16 // PIECES, 16 // PIECES)
         return (
@@ -725,27 +754,30 @@
             pltpu.make_async_copy(held.at[n, at], dst.at[at], sems.at[1, n, m]),
         )
 
+    take_terms = pltpu.make_async_copy(total, terms, more.at[0])
+    give_weights = pltpu.make_async_copy(weights, weight_out, more.at[1])
     pieces = [
         piece(n, m, src, dst)
         for n, (src, dst) in enumerate(((act, act_out), (grad, grad_out)))
         for m in range(PIECES)
     ]
+    take_terms.start()
     for take, _ in pieces:
         take.start()
+    take_terms.wait()
+    for n in range(27):
+        weights[n % 3 * 9 + n // 3] = terms[n * CH : (n + 1) * CH].astype(F32)
+    bias_out[...] = terms[27 * CH : 27 * CH + 16].astype(F32)[0:1]
+    give_weights.start()
     for take, give in pieces:
         take.wait()
         give.start()
-    for n in range(28):
-        total, at = (total_a, n * CH) if n < PARTS[1][0] else (total_b, (n - PARTS[1][0]) * CH)
-        if n < 27:
-            weight_out[n % 3 * 9 + n // 3] = total[at : at + CH].astype(F32)
-        else:
-            bias_out[...] = total[at : at + 16].astype(F32)[0:1]
     for _, give in pieces:
         give.wait()
-
-
-def deliver(act, grad, total_a, total_b):
+    give_weights.wait()
+
+
+def deliver(act, grad, total):
     vm = pl.BlockSpec(memory_space=pltpu.VMEM)
     hbm = pl.BlockSpec(memory_space=pl.ANY)
     return pl.pallas_call(
@@ -756,19 +788,22 @@
             jax.ShapeDtypeStruct((27, CH, CH), F32),
             jax.ShapeDtypeStruct((1, CH), F32),
         ),
-        in_specs=[hbm, hbm, vm, vm],
-        out_specs=(hbm, hbm, vm, vm),
+        in_specs=[hbm, hbm, hbm],
+        out_specs=(hbm, hbm, hbm, vm),
         scratch_shapes=[
             pltpu.VMEM((2, 16, 512, CH), BF16),
+            pltpu.VMEM((ROWS, CH), BF16),
+            pltpu.VMEM((27, CH, CH), F32),
             pltpu.SemaphoreType.DMA((2, 2, PIECES)),
+            pltpu.SemaphoreType.DMA((2,)),
         ],
         compiler_params=pltpu.CompilerParams(vmem_limit_bytes=63 * 2**20),
         name="deliver",
-    )(act, grad, total_a, total_b)
+    )(act, grad, total)
 
 
 def shards(features, cotangent, kernel_weight, conv_bias, send_lists, kernel_map):
-    act, grad, total_a, total_b = layer(
+    act, grad, total = layer(
         features.reshape(16, 512, CH),
         cotangent.reshape(16, 512, CH),
         kernel_weight.reshape(27, CH, CH),
@@ -776,9 +811,7 @@
         send_lists[0, 0].T,
         kernel_map[0, 0],
     )
-    act, grad, weight_total, bias_total = deliver(
-        act, grad, total_a.reshape(-1, CH), total_b.reshape(-1, CH)
-    )
+    act, grad, weight_total, bias_total = deliver(act, grad, total.reshape(ROWS, CH))
     return (
         act.reshape(features.shape),
         grad.reshape(features.shape),

time: 93.1 us -> 90.4 us (0.971)
  Pallas kernels: 92 us -> 89.4 us
    pallas_call x1, Pallas kernels: 86.1 us -> 83.8 us  [layer(): pl.pallas_call(kernel, out_shape=(jax.ShapeDtypeStruct((16, 512, CH), BF1...]
where the time goes in v5:
time: 90.4 us; the launch traced here: 90.3 us
  Pallas kernels  89.4 us (99%)
    pallas_call x1, Pallas kernels, layer(): pl.pallas_call(kernel, out_shape=(jax.ShapeDtypeStruct((16, 512, CH), BF1...  83.8 us
    pallas_call x1, Pallas kernels, deliver(): pl.pallas_call(deliver_kernel, out_shape=(jax.ShapeDtypeStruct(act.shape,...  5.62 us

profile of v5, /device:TPU:1, one launch (start us, length us, event | category | flops | bytes accessed | tf_op | source)
XLA Modules:
  0.0 90.3 jit_solution(7510946415324243136)
XLA Ops:
  0.6 83.8 %layer.1 = (bf16[16,512,128]{2,1,0:T(8,128)(2,1)}, bf16[16,512,128]{2,1,0:T(8,128)(2,1)}, bf16[2,16,112,128]{3,2,1,0:T(8,128)(2,1)}) custom-call(bf16[16,512,128]{2,1,0:T(8,128)(2,1)} %bitcast.13, bf16[16,512,128]{2,1,0:T(8,128)(2,1)} %bitcast.14, bf16[27,128,128]{2,1,0:T(8,128)(2,1)} %bitcast.16, f32[1,128]{1,0:T(1,128)} %bitcast.19, s32[4,8]{1,0:T(4,128)} %bitcast.18, ...), custom_call_target="tpu_custom_call" | custom-call | tf_op jit(solution)/shard_map/layer/pallas_call | solution.py:703
  84.5 5.6 %deliver.1 = (bf16[16,512,128]{2,1,0:T(8,128)(2,1)}, bf16[16,512,128]{2,1,0:T(8,128)(2,1)}, f32[27,128,128]{2,1,0:T(8,128)}, f32[1,128]{1,0:T(1,128)}) custom-call(bf16[16,512,128]{2,1,0:T(8,128)(2,1)} %get-tuple-element.11.act, bf16[16,512,128]{2,1,0:T(8,128)(2,1)} %get-tuple-element.12.grad, bf16[3584,128]{1,0:T(8,128)(2,1)} %bitcast.15), custom_call_target="tpu_custom_call" | custom-call | tf_op jit(solution)/shard_map/deliver/pallas_call | solution.py:783

commit v6 on v5

--- a/solution.py
+++ b/solution.py
@@ -311,14 +311,18 @@
             sending[k, r] = faces[jnp.minimum(lists[r, k], 15)]
 
 
-def halo_copy(k, sending, received, send_sem, recv_sem):
+SENDINGS = ((0, 2), (2, 1), (3, 1))
+
+
+def halo_copy(k, m, sending, received, send_sem, recv_sem):
     i, j = lax.axis_index("gx"), lax.axis_index("gy")
     dx, dy = DIRECTIONS[k]
+    slots = pl.ds(*SENDINGS[m])
     return pltpu.make_async_remote_copy(
-        src_ref=sending.at[k],
-        dst_ref=received.at[k],
-        send_sem=send_sem.at[k],
-        recv_sem=recv_sem.at[k],
+        src_ref=sending.at[k, slots],
+        dst_ref=received.at[k, slots],
+        send_sem=send_sem.at[m, k],
+        recv_sem=recv_sem.at[m, k],
         device_id=(i + dx, j + dy),
         device_id_type=MESH,
     )
@@ -327,14 +331,15 @@
 ORDER = (0, 2, 5, 7, 3, 4, 1, 6)
 
 
-def start_halo(*halo):
+def start_halo(parts, *halo):
     i, j = lax.axis_index("gx"), lax.axis_index("gy")
     for k in ORDER:
         dx, dy = DIRECTIONS[k]
 
         @pl.when(inside(i + dx, j + dy))
         def _():
-            halo_copy(k, *halo).start()
+            for m in parts:
+                halo_copy(k, m, *halo).start()
 
 
 def wait_halo(*halo):
@@ -344,7 +349,8 @@
 
         @pl.when(inside(i - dx, j - dy))
         def _():
-            halo_copy(k, *halo).wait_recv()
+            for m in range(3):
+                halo_copy(k, m, *halo).wait_recv()
 
 
 def wait_halo_sent(*halo):
@@ -354,7 +360,8 @@
 
         @pl.when(inside(i + dx, j + dy))
         def _():
-            halo_copy(k, *halo).wait_send()
+            for m in range(3):
+                halo_copy(k, m, *halo).wait_send()
 
 
 BLOCKS = 28
@@ -610,7 +617,7 @@
     own_table(x32, t32, faces)
     pack_lists(lists, faces, sending)
     pl.semaphore_wait(barrier, neighbours + summers)
-    start_halo(*halo)
+    start_halo((0, 1, 2), *halo)
 
     def put_x(a, e, c, v):
         x[1 + a, 1 + e, 1 + c] = v
@@ -651,7 +658,7 @@
     own_table(x32, t32, faces)
     pack_lists(lists, faces, sending)
     pl.semaphore_wait(credit, neighbours)
-    start_halo(*halo)
+    start_halo((0,), *halo)
 
     def turn(p, sums):
         for m in range(8):
@@ -674,8 +681,10 @@
     give_act.start()
     wide_weights(w, w2, wa, True)
     terms_sum.start_plane()
+    start_halo((1,), *halo)
     inner_conv(g, w2, wa, lin, 0, 3)
     terms_sum.start_column()
+    start_halo((2,), *halo)
     inner_conv(g, w2, wa, lin, 3, 4)
     terms_sum.start_back()
     wait_halo(*halo)
@@ -728,8 +737,8 @@
             pltpu.VMEM((2, 12 * CH, 2 * CH), BF16),
             pltpu.VMEM((4, 2 * CH, 1024), BF16),
             pltpu.VMEM((ROWS, CH), F32),
-            pltpu.SemaphoreType.DMA((8,)),
-            pltpu.SemaphoreType.DMA((8,)),
+            pltpu.SemaphoreType.DMA((3, 8)),
+            pltpu.SemaphoreType.DMA((3, 8)),
             pltpu.SemaphoreType.DMA((5,)),
             pltpu.SemaphoreType.REGULAR,
             *sum_scratch(BLOCKS),

time: 90.4 us -> 91.7 us (1.014)
  Pallas kernels: 89.4 us -> 90.7 us
    pallas_call x1, Pallas kernels: 83.8 us -> 85.1 us  [layer(): pl.pallas_call(kernel, out_shape=(jax.ShapeDtypeStruct((16, 512, CH), BF1...]
where the time goes in v6:
time: 91.7 us; the launch traced here: 91.5 us
  Pallas kernels  90.7 us (99%)
    pallas_call x1, Pallas kernels, layer(): pl.pallas_call(kernel, out_shape=(jax.ShapeDtypeStruct((16, 512, CH), BF1...  85.1 us
    pallas_call x1, Pallas kernels, deliver(): pl.pallas_call(deliver_kernel, out_shape=(jax.ShapeDtypeStruct(act.shape,...  5.62 us

profile of v6, /device:TPU:1, one launch (start us, length us, event | category | flops | bytes accessed | tf_op | source)
XLA Modules:
  0.0 91.5 jit_solution(15244104638007398839)
XLA Ops:
  0.6 85.1 %layer.1 = (bf16[16,512,128]{2,1,0:T(8,128)(2,1)}, bf16[16,512,128]{2,1,0:T(8,128)(2,1)}, bf16[2,16,112,128]{3,2,1,0:T(8,128)(2,1)}) custom-call(bf16[16,512,128]{2,1,0:T(8,128)(2,1)} %bitcast.13, bf16[16,512,128]{2,1,0:T(8,128)(2,1)} %bitcast.14, bf16[27,128,128]{2,1,0:T(8,128)(2,1)} %bitcast.16, f32[1,128]{1,0:T(1,128)} %bitcast.19, s32[4,8]{1,0:T(4,128)} %bitcast.18, ...), custom_call_target="tpu_custom_call" | custom-call | tf_op jit(solution)/shard_map/layer/pallas_call | solution.py:712
  85.7 5.6 %deliver.1 = (bf16[16,512,128]{2,1,0:T(8,128)(2,1)}, bf16[16,512,128]{2,1,0:T(8,128)(2,1)}, f32[27,128,128]{2,1,0:T(8,128)}, f32[1,128]{1,0:T(1,128)}) custom-call(bf16[16,512,128]{2,1,0:T(8,128)(2,1)} %get-tuple-element.11.act, bf16[16,512,128]{2,1,0:T(8,128)(2,1)} %get-tuple-element.12.grad, bf16[3584,128]{1,0:T(8,128)(2,1)} %bitcast.15), custom_call_target="tpu_custom_call" | custom-call | tf_op jit(solution)/shard_map/deliver/pallas_call | solution.py:792

commit v7 on v5

--- a/solution.py
+++ b/solution.py
@@ -78,10 +78,10 @@
     lax.fori_loop(0, 16, one, 0)
 
 
-def received_table(received, t32, wide):
-    def one(n, _):
+def received_table(k, received, t32, wide):
+    def one(r, _):
+        n = 4 * k + r
         base = (16 + n) * ENTRY
-        k, r = n // 4, n % 4
         sides = received[k, r, 0:128].astype(F32)
         wide[0:128] = sides
         t32[pl.ds(base, 16)] = sides.reshape(16, 8, CH)
@@ -102,8 +102,7 @@
             t32[base + EDGES + m] = wide[pl.ds(start, 8, stride=8)]
         return 0
 
-    lax.fori_loop(0, 32, one, 0)
-    t32[pl.ds(48 * ENTRY, ENTRY)] = jnp.zeros((ENTRY, 8, CH), F32)
+    lax.fori_loop(0, 4, one, 0)
 
 
 def rim(kmap, t32, x32, planes, x):
@@ -337,14 +336,17 @@
             halo_copy(k, *halo).start()
 
 
-def wait_halo(*halo):
+def take_halo(t32, wide, *halo):
     i, j = lax.axis_index("gx"), lax.axis_index("gy")
-    for k in ORDER:
+    t32[pl.ds(48 * ENTRY, ENTRY)] = jnp.zeros((ENTRY, 8, CH), F32)
+    for k in (1, 6, 0, 2, 5, 7, 3, 4):
         dx, dy = DIRECTIONS[k]
 
         @pl.when(inside(i - dx, j - dy))
         def _():
             halo_copy(k, *halo).wait_recv()
+
+        received_table(k, halo[1], t32, wide)
 
 
 def wait_halo_sent(*halo):
@@ -626,8 +628,7 @@
     wide_weights(w, w2, wa, False)
     clear_rims(planes, x, g)
     inner_conv(x, w2, wa, lin, 0, 4)
-    wait_halo(*halo)
-    received_table(received, t32, wide)
+    take_halo(t32, wide, *halo)
     credit_neighbours(credit)
     rim(kmap, t32, x32, planes, x)
     rim_conv(planes, w2, wa, lin)
@@ -678,8 +679,7 @@
     terms_sum.start_column()
     inner_conv(g, w2, wa, lin, 3, 4)
     terms_sum.start_back()
-    wait_halo(*halo)
-    received_table(received, t32, wide)
+    take_halo(t32, wide, *halo)
     rim(kmap, t32, x32, planes, None)
     rim_conv(planes, w2, wa, lin)
     terms_sum.start_last()

time: 90.4 us -> 89.6 us (level)
  no operation moved by 1% of the time
where the time goes in v7:
time: 89.6 us; the launch traced here: 89.4 us
  Pallas kernels  88.6 us (99%)
    pallas_call x1, Pallas kernels, layer(): pl.pallas_call(kernel, out_shape=(jax.ShapeDtypeStruct((16, 512, CH), BF1...  83 us
    pallas_call x1, Pallas kernels, deliver(): pl.pallas_call(deliver_kernel, out_shape=(jax.ShapeDtypeStruct(act.shape,...  5.62 us

profile of v7, /device:TPU:1, one launch (start us, length us, event | category | flops | bytes accessed | tf_op | source)
XLA Modules:
  0.0 89.4 jit_solution(162479852088971446)
XLA Ops:
  0.6 83.0 %layer.1 = (bf16[16,512,128]{2,1,0:T(8,128)(2,1)}, bf16[16,512,128]{2,1,0:T(8,128)(2,1)}, bf16[2,16,112,128]{3,2,1,0:T(8,128)(2,1)}) custom-call(bf16[16,512,128]{2,1,0:T(8,128)(2,1)} %bitcast.13, bf16[16,512,128]{2,1,0:T(8,128)(2,1)} %bitcast.14, bf16[27,128,128]{2,1,0:T(8,128)(2,1)} %bitcast.16, f32[1,128]{1,0:T(1,128)} %bitcast.19, s32[4,8]{1,0:T(4,128)} %bitcast.18, ...), custom_call_target="tpu_custom_call" | custom-call | tf_op jit(solution)/shard_map/layer/pallas_call | solution.py:703
  83.6 5.6 %deliver.1 = (bf16[16,512,128]{2,1,0:T(8,128)(2,1)}, bf16[16,512,128]{2,1,0:T(8,128)(2,1)}, f32[27,128,128]{2,1,0:T(8,128)}, f32[1,128]{1,0:T(1,128)}) custom-call(bf16[16,512,128]{2,1,0:T(8,128)(2,1)} %get-tuple-element.11.act, bf16[16,512,128]{2,1,0:T(8,128)(2,1)} %get-tuple-element.12.grad, bf16[3584,128]{1,0:T(8,128)(2,1)} %bitcast.15), custom_call_target="tpu_custom_call" | custom-call | tf_op jit(solution)/shard_map/deliver/pallas_call | solution.py:783
